TPU v7x, 128 devices: a whole 4x4x4 slice. The times are simulated.
128 devices in a mesh: head: 4 (over x_lo, core), outer: 2 (over x_hi), inner: 16 (over z, y).
Axes of the slice: x: 4 (x_hi: 2, x_lo: 2; x = x_hi * 2 + x_lo), y: 4, z: 4, core: 2. Of those that a mesh axis runs over, the one named last changes fastest.
Arguments:
- queries: bfloat16 [8192, 8192], P(('outer', 'inner'), 'head'), may hold values from -128 to 128
- keys: bfloat16 [8192, 1024], P(('outer', 'inner'), 'head'), may hold values from -6 to 6
- values: bfloat16 [8192, 1024], P(('outer', 'inner'), 'head'), may hold values from -6 to 6
- segment_ids: int32 [8192], P(('outer', 'inner')), may hold values from 0 to 7, never falling along the last dimension, each value on 1 to 6144 neighbouring positions
- value_weight: float32 [8192], P('head'), may hold values from -0.3 to 0.3
- targets: float32 [8192], P(('outer', 'inner')), may hold values from -6 to 6
- upstream: bfloat16 [8192, 8192], P(('outer', 'inner'), 'head'), may hold values from -6 to 6
Outputs:
- query_grad: bfloat16 [8192, 8192], P(('outer', 'inner'), 'head')
- key_grad: bfloat16 [8192, 1024], P(('outer', 'inner'), 'head')
- value_grad: bfloat16 [8192, 1024], P(('outer', 'inner'), 'head')
- value_error: float32 [8192], P(('outer', 'inner'))
- readout_grad: float32 [8192], P('head')
Inputs may be any that keep to these rules, and one draw needn't show every extreme that they name: `segment_ids`: segment numbers never fall along the tokens; a segment holds at most 6144 tokens, and one holds exactly that many.
All inputs are finite; a program needn't handle non-finite values.
Results may differ from a plain program's by a relative error of at most 0.027.
Values may be sent and summed in bfloat16 or wider, within the bound.
No kernel may reach another device: no remote copies, remote signals or barrier semaphores. Data moves between devices by JAX's collectives and lax.ppermute only.
A program may use at most 448 MiB of HBM per device.

v0:
```python
import functools
import math

import jax
import jax.numpy as jnp
from jax import lax
from jax.experimental import pallas as pl
from jax.experimental.pallas import tpu as pltpu
from jax.sharding import PartitionSpec as P

HD = 128
BLK = 256
NB = 32
HPD = 4
WIDTH = HPD * HD
PAD = 16
LINE = 4 * HD
TILE = 4
SCALE = HD ** (-0.5)
SCALE2 = SCALE * math.log2(math.e)
NEG = -1e30
CTX = ("outer", "zh", "zl", "y")
GROUP = ("outer", "zh")
NT = (((1,), (1,)), ((), ()))
F32 = jnp.float32
BF16 = jnp.bfloat16
VMEM_LIMIT = 52 * 1024 * 1024


def dot(a, b):
    return jnp.dot(a, b, preferred_element_type=F32)


def dot_nt(a, b):
    return lax.dot_general(a, b, NT, preferred_element_type=F32)


def rows(b, n=1):
    return pl.ds(pl.multiple_of(b * BLK, BLK), n * BLK)


def block_of(scal, o, dz, dy):
    z = (scal[12] + dz) & 3
    y = (scal[13] + dy) & 3
    return 16 * o + 4 * z + y


def place(scal, pieces, z_first, put):
    for far in range(4):
        for near in range(4):
            for o in range(2):
                dz, dy = (near, far) if z_first else (far, near)
                put(block_of(scal, 0, dz, dy), o, pieces[far][near, o, :BLK, :])


def start_of(scal, pos):
    lo = jnp.zeros_like(pos)
    for v in range(1, 8):
        lo = jnp.maximum(lo, jnp.where(pos >= scal[v], scal[v], 0))
    return lo


def allowed_of(scal, base, kb):
    query_pos = base + lax.broadcasted_iota(jnp.int32, (1, BLK), 1)
    lo = start_of(scal, query_pos)
    key_pos = kb * BLK + lax.broadcasted_iota(jnp.int32, (BLK, BLK), 0)
    return (key_pos <= query_pos) & (key_pos >= lo)


def sweep(scal, base, low, high, tile, body):
    diag = base // BLK
    first = start_of(scal, base) // BLK
    full = jnp.minimum((start_of(scal, base + BLK - 1) + BLK - 1) // BLK, diag)
    stop = jnp.clip(diag, low, high)
    full = jnp.clip(full, low, stop)
    first = jnp.clip(first, low, full)

    @pl.when((diag >= low) & (diag < high))
    def _():
        body(diag, 1, True)

    def masked(kb, c):
        body(kb, 1, True)
        return c

    def plain(t, c):
        body(full + tile * t, tile, False)
        return c

    def single(kb, c):
        body(kb, 1, False)
        return c

    count = (stop - full) // tile
    lax.fori_loop(first, full, masked, 0)
    lax.fori_loop(0, count, plain, 0)
    lax.fori_loop(full + tile * count, stop, single, 0)


def largest_norm(blocks):
    ones = jnp.ones((8, HD), BF16)
    most = jnp.zeros((8, BLK), F32)
    for x in blocks:
        most = jnp.maximum(most, dot_nt(ones, x * x))
    return jnp.max(most) * 1.02


def forward_kernel(
    scal, q_ref, k0, k1, k2, k3, v0, v1, v2, v3, w_ref,
    out_ref, lse_ref, critic_ref, qt_ref,
    k_all, vt_all, qt_all, acc, top, tot, flag,
):
    p = pl.program_id(0)

    @pl.when(p == 0)
    def _():
        norms = []
        for piece in range(4):
            for h in range(HPD):
                x = q_ref[piece, :, h * HD:(h + 1) * HD]
                qt_all[piece, h] = x.T
                norms.append(x)
        query_norm = largest_norm(norms)
        norms = []

        def put_k(b, o, blk):
            k_all[rows(b + 16 * o), :] = blk
            norms.append(blk)

        def put_v(b, o, blk):
            vt_all[b + 16 * o] = blk.T

        place(scal, (k0, k1, k2, k3), True, put_k)
        place(scal, (v0, v1, v2, v3), False, put_v)
        small = query_norm * largest_norm(norms) * SCALE2 * SCALE2 <= 3600.0
        flag[0] = small.astype(jnp.int32)

    small = flag[0] == 1
    base = scal[8 + p]
    tot[...] = jnp.zeros_like(tot)
    acc[...] = jnp.zeros_like(acc)
    for h in range(HPD):
        qt_ref[0, h] = qt_all[p, h]

    def values_of(kb, n):
        return jnp.concatenate([vt_all[kb + t] for t in range(n)], 1)

    def bounded(kb, n, masked):
        k_blk = k_all[rows(kb, n), :]
        vt_blk = values_of(kb, n)
        if masked:
            allowed = allowed_of(scal, base, kb)
        ss = [dot(k_blk, qt_all[p, h]) for h in range(HPD)]
        probs = [jnp.exp2(s * SCALE2) for s in ss]
        if masked:
            probs = [jnp.where(allowed, x, 0.0) for x in probs]
        pv = [dot(vt_blk, x.astype(BF16)) for x in probs]
        tots = [tot[h] + jnp.sum(probs[h], 0, keepdims=True) for h in range(HPD)]
        accs = [acc[h] + pv[h] for h in range(HPD)]
        for h in range(HPD):
            tot[h] = tots[h]
            acc[h] = accs[h]

    def general(kb, n, masked):
        k_blk = k_all[rows(kb, n), :]
        vt_blk = values_of(kb, n)
        ss = [dot(k_blk, qt_all[p, h]) for h in range(HPD)]
        if masked:
            allowed = allowed_of(scal, base, kb)
            ss = [jnp.where(allowed, s, NEG) for s in ss]
        olds = [top[h] for h in range(HPD)]
        news = [jnp.maximum(olds[h], jnp.max(ss[h], 0, keepdims=True)) for h in range(HPD)]
        probs = [jnp.exp2(ss[h] * SCALE2 - news[h] * SCALE2) for h in range(HPD)]
        fades = [jnp.exp2((olds[h] - news[h]) * SCALE2) for h in range(HPD)]
        pv = [dot(vt_blk, x.astype(BF16)) for x in probs]
        tots = [tot[h] * fades[h] + jnp.sum(probs[h], 0, keepdims=True) for h in range(HPD)]
        accs = [acc[h] * fades[h] + pv[h] for h in range(HPD)]
        for h in range(HPD):
            top[h] = news[h]
            tot[h] = tots[h]
            acc[h] = accs[h]

    @pl.when(small)
    def _():
        top[...] = jnp.zeros_like(top)
        sweep(scal, base, 0, NB, TILE, bounded)

    @pl.when(jnp.logical_not(small))
    def _():
        top[...] = jnp.full_like(top, NEG)
        sweep(scal, base, 0, NB, TILE, general)

    critic = jnp.zeros((1, BLK), F32)
    for h in range(HPD):
        total = tot[h]
        out = (acc[h] / total).astype(BF16)
        out_ref[0, h] = out
        lse_ref[0, h] = top[h] * SCALE2 + jnp.log2(total)
        w = w_ref[h * HD:(h + 1) * HD, :]
        critic += jnp.sum(out.astype(F32) * jnp.concatenate([w, w], 1), 0, keepdims=True)
    critic_ref[0] = critic


def prepare_kernel(
    scal, u_ref, k0, k1, k2, k3, v0, v1, v2, v3,
    ut_ref, k_low, k_high, kt_low, kt_high, vt_low, vt_high,
):
    for p in range(4):
        for h in range(HPD):
            ut_ref[p, h] = u_ref[p, :, h * HD:(h + 1) * HD].T

    def put_k(b, o, blk):
        (k_low, k_high)[o][rows(b), :] = blk
        (kt_low, kt_high)[o][b] = blk.T

    def put_v(b, o, blk):
        (vt_low, vt_high)[o][b] = blk.T

    place(scal, (k0, k1, k2, k3), True, put_k)
    place(scal, (v0, v1, v2, v3), False, put_v)


def spread(row):
    return jnp.broadcast_to(row, (HD, BLK)).T


def allowed_by_row(scal, base, kb):
    query_pos = base + lax.broadcasted_iota(jnp.int32, (BLK, HD), 0)
    lo = start_of(scal, query_pos)
    key_pos = kb * BLK + lax.broadcasted_iota(jnp.int32, (BLK, HD), 1)
    halves = [(x <= query_pos) & (x >= lo) for x in (key_pos, key_pos + HD)]
    return halves


def gradients(scal, low, high, q_ref, qt_ref, k_ref, kt_ref, vt_ref, do_s, dot_ref, lse_s, delta_s, dkt, dvt, dq):
    base = scal[8 + pl.program_id(0)]

    def body(kb, n, masked):
        at = kb - low
        k_blk = k_ref[rows(at, n), :]
        kt_blk = jnp.concatenate([kt_ref[at + t] for t in range(n)], 1)
        vt_blk = jnp.concatenate([vt_ref[at + t] for t in range(n)], 1)
        ss = [dot(q_ref[0, :, h * HD:(h + 1) * HD], kt_blk) for h in range(HPD)]
        dps = [dot(do_s[h], vt_blk) for h in range(HPD)]
        lses = [jnp.concatenate([lse_s[h]] * (2 * n), 1) for h in range(HPD)]
        deltas = [jnp.concatenate([delta_s[h]] * (2 * n), 1) for h in range(HPD)]
        probs = [jnp.exp2(ss[h] * SCALE2 - lses[h]) for h in range(HPD)]
        if masked:
            left, right = allowed_by_row(scal, base, kb)
            probs = [
                jnp.concatenate([jnp.where(left, x[:, :HD], 0.0), jnp.where(right, x[:, HD:], 0.0)], 1)
                for x in probs
            ]
        dls = [(probs[h] * (dps[h] - deltas[h])).astype(BF16) for h in range(HPD)]
        dv = sum(dot(dot_ref[0, h], probs[h].astype(BF16)) for h in range(HPD))
        dk = sum(dot(qt_ref[0, h], dls[h]) for h in range(HPD))
        upd = [dq[h] + dot(dls[h], k_blk) for h in range(HPD)]
        for h in range(HPD):
            dq[h] = upd[h]
        for t in range(n):
            span = slice(t * BLK, (t + 1) * BLK)
            dkt[at + t] += dk[:, span]
            dvt[at + t] += dv[:, span]

    sweep(scal, base, low, high, TILE, body)


def key_sum(dkt, b):
    return (dkt[b] * SCALE).astype(BF16)


def value_sum(dvt, b):
    return dvt[b].astype(BF16)


def upper_kernel(
    scal, q_ref, ut_ref, qt_ref, k_ref, kt_ref, vt_ref, w_ref, out_ref, lse_ref, err_ref,
    part_ref, dot_ref, delta_ref, line0, line1, line2, line3,
    dkt, dvt, dq, do_s, lse_s, delta_s, readout, readout_all,
):
    p = pl.program_id(0)

    @pl.when(p == 0)
    def _():
        dkt[...] = jnp.zeros_like(dkt)
        dvt[...] = jnp.zeros_like(dvt)
        readout[...] = jnp.zeros_like(readout)

    dq[...] = jnp.zeros_like(dq)
    err = err_ref[0]
    for h in range(HPD):
        w = w_ref[h * HD:(h + 1) * HD, :]
        w = jnp.concatenate([w, w], 1)
        out = out_ref[0, h].astype(F32)
        dout = (err * w + ut_ref[0, h].astype(F32)).astype(BF16)
        delta = jnp.sum(dout.astype(F32) * out, 0, keepdims=True)
        dot_ref[0, h] = dout
        delta_ref[0, h] = delta
        do_s[h] = dout.T
        delta_s[h] = spread(delta)
        lse_s[h] = spread(lse_ref[0, h])
        readout[h] += err * out
    gradients(
        scal, NB // 2, NB, q_ref, qt_ref, k_ref, kt_ref, vt_ref, do_s, dot_ref, lse_s, delta_s, dkt, dvt, dq
    )
    part_ref[0] = dq[...].astype(BF16)

    @pl.when(p == 3)
    def _():
        readout_all[...] = jnp.zeros_like(readout_all)
        lanes = [jnp.sum(readout[h].T, 0, keepdims=True) for h in range(HPD)]
        for r in range(2):
            readout_all[pl.ds(2 * scal[14] + r, 1), :] = jnp.concatenate(lanes[2 * r:2 * r + 2], 1)
        high = readout_all[...].astype(BF16).astype(F32)
        tail = jnp.concatenate([high, readout_all[...] - high], 0).astype(BF16)
        for dy, line in enumerate((line0, line1, line2, line3)):
            for dz in range(4):
                b = block_of(scal, 0, dz, dy)
                line[2 * dz * HD:(2 * dz + 1) * HD, :] = key_sum(dkt, b)
                line[(2 * dz + 1) * HD:(2 * dz + 2) * HD, :] = value_sum(dvt, b)
            line[2 * LINE:, :] = tail


def lower_kernel(
    scal, q_ref, qt_ref, k_ref, kt_ref, vt_ref, dot_ref, lse_ref, delta_ref, part_ref,
    dq_ref, dk0, dk1, dk2, dk3, dv0, dv1, dv2, dv3,
    dkt, dvt, dq, do_s, lse_s, delta_s,
):
    p = pl.program_id(0)

    @pl.when(p == 0)
    def _():
        dkt[...] = jnp.zeros_like(dkt)
        dvt[...] = jnp.zeros_like(dvt)

    for h in range(HPD):
        do_s[h] = dot_ref[0, h].T
        delta_s[h] = spread(delta_ref[0, h])
        lse_s[h] = spread(lse_ref[0, h])
    dq[...] = part_ref[0].astype(F32)
    gradients(
        scal, 0, NB // 2, q_ref, qt_ref, k_ref, kt_ref, vt_ref, do_s, dot_ref, lse_s, delta_s, dkt, dvt, dq
    )
    for h in range(HPD):
        dq_ref[0, :, h * HD:(h + 1) * HD] = (dq[h] * SCALE).astype(BF16)

    @pl.when(p == 3)
    def _():
        for far, (dk, dv) in enumerate(((dk0, dv0), (dk1, dv1), (dk2, dv2), (dk3, dv3))):
            for near in range(4):
                span = slice(near * HD, (near + 1) * HD)
                dk[span, :] = key_sum(dkt, block_of(scal, 0, near, far))
                dv[span, :] = value_sum(dvt, block_of(scal, 0, far, near))


SMEM_SPEC = pl.BlockSpec(memory_space=pltpu.SMEM)
VMEM_SPEC = pl.BlockSpec(memory_space=pltpu.VMEM)


def by_piece(shape):
    return pl.BlockSpec((1, *shape[1:]), lambda p: (p,) + (0,) * (len(shape) - 1))


def call(kernel, name, shapes, scratch, flops, split, part, *args):
    shapes = [jax.ShapeDtypeStruct(shape, kind) for shape, kind in shapes]
    every = [*args, *shapes]
    specs = [SMEM_SPEC] + [
        by_piece(every[t].shape) if t in split else VMEM_SPEC for t in range(1, len(every))
    ]
    if part is not None:
        specs[1] = part
    return pl.pallas_call(
        kernel,
        grid=(4 if split else 1,),
        out_shape=tuple(shapes),
        in_specs=specs[:len(args)],
        out_specs=tuple(specs[len(args):]),
        scratch_shapes=[
            pltpu.SMEM((1,), jnp.int32) if kind is None else pltpu.VMEM(shape, kind) for shape, kind in scratch
        ],
        compiler_params=pltpu.CompilerParams(vmem_limit_bytes=VMEM_LIMIT),
        cost_estimate=pl.CostEstimate(flops=flops, bytes_accessed=8 << 20, transcendentals=10**6),
        name=name,
    )(*args)


ALL_QUERIES = pl.BlockSpec((4, BLK, WIDTH), lambda p: (0, 0, 0))
ALL_UPSTREAM = pl.BlockSpec((4, BLK, WIDTH), lambda p: (0, 1, 0))
ONE_QUERIES = pl.BlockSpec((1, BLK, WIDTH), lambda p: (p, 0, 0))
HEADS = (4, HPD, HD, BLK)
STATS = (4, HPD, 1, BLK)
PIECES = (4, BLK, WIDTH)
COLUMNS = ((HPD, BLK, HD), F32)
HALF = ((NB // 2 * BLK, HD), BF16)
HALF_T = ((NB // 2, HD, BLK), BF16)
SUMS = ((NB // 2, HD, BLK), F32)


def forward(scal, qu, kp, vp, w):
    return call(
        forward_kernel, "attention_forward",
        [(HEADS, BF16), (STATS, F32), ((4, 1, BLK), F32), (HEADS, BF16)],
        [
            ((NB * BLK, HD), BF16), ((NB, HD, BLK), BF16), (HEADS, BF16),
            (HEADS[1:], F32), (STATS[1:], F32), (STATS[1:], F32), ((1,), None),
        ],
        9 * 10**9, (11, 12, 13, 14), ALL_QUERIES, scal, qu, *kp, *vp, w,
    )


def prepare(scal, qu, kp, vp):
    return call(
        prepare_kernel, "prepare_backward",
        [(HEADS, BF16), HALF, HALF, HALF_T, HALF_T, HALF_T, HALF_T],
        [], 10**8, (), ALL_UPSTREAM, scal, qu, *kp, *vp,
    )


def upper(scal, qu, ut, qt, k, kt, vt, w, out, lse, err):
    return call(
        upper_kernel, "attention_upper",
        [((4, HPD, BLK, HD), BF16), (HEADS, BF16), (STATS, F32)]
        + [((2 * LINE + 16, BLK), BF16)] * 4,
        [SUMS, SUMS, COLUMNS, ((HPD, BLK, HD), BF16), COLUMNS, COLUMNS, (HEADS[1:], F32), ((8, BLK), F32)],
        8 * 10**9, (2, 3, 8, 9, 10, 11, 12, 13), ONE_QUERIES, scal, qu, ut, qt, k, kt, vt, w, out, lse, err,
    )


def lower(scal, qu, qt, k, kt, vt, dout, lse, delta, part):
    return call(
        lower_kernel, "attention_lower",
        [(PIECES, BF16)] + [((LINE, BLK), BF16)] * 8,
        [SUMS, SUMS, COLUMNS, ((HPD, BLK, HD), BF16), COLUMNS, COLUMNS],
        16 * 10**9, (2, 6, 7, 8, 9, 10), ONE_QUERIES, scal, qu, qt, k, kt, vt, dout, lse, delta, part,
    )


def send(x, move):
    pairs = []
    for b in range(NB):
        o, z, y = move(b // 16, b // 4 % 4, b % 4)
        pairs.append((b, 16 * o + 4 * (z % 4) + y % 4))
    return lax.ppermute(x, CTX, pairs)


def swap(x, k):
    return send(x, lambda o, z, y: (o ^ (k >> 1), z ^ (2 * (k & 1)), y))


def trade(x):
    return lax.all_to_all(x, GROUP, 0, 0, tiled=True)


def quarters(x):
    return jnp.stack([x[:, m * WIDTH:(m + 1) * WIDTH] for m in range(4)])


def from_z(x, d):
    return send(x, lambda o, z, y: (o, z - d, y))


def from_y(x, d):
    return send(x, lambda o, z, y: (o, z, y - d))


def to_z(x, d):
    return send(x, lambda o, z, y: (o, z + d, y))


def to_y(x, d):
    return send(x, lambda o, z, y: (o, z, y + d))


def halves(x):
    high = lax.reduce_precision(x, 8, 7)
    return jnp.concatenate([high, x - high], 0).astype(BF16)


def joined(x):
    return x[:8] + x[8:]


def total_of(parts):
    return functools.reduce(jnp.add, [x.astype(F32) for x in parts])


def local(queries, keys, values, segment_ids, value_weight, targets, upstream):
    o = lax.axis_index("outer")
    head = lax.axis_index("head")
    z, y = 2 * lax.axis_index("zh") + lax.axis_index("zl"), lax.axis_index("y")
    member = lax.axis_index(GROUP)

    below = jnp.sum(
        segment_ids[:, None] < jnp.arange(HD, dtype=jnp.int32)[None, :], 0, dtype=jnp.int32
    )
    below = jnp.where(jnp.arange(HD) < 8, below, 0).astype(F32).astype(BF16)
    pad = jnp.concatenate([below[None, :], jnp.zeros((PAD - 1, HD), BF16)], 0)

    def packed(index):
        k = lax.dynamic_slice_in_dim(keys, index * HD, HD, 1)
        v = lax.dynamic_slice_in_dim(values, index * HD, HD, 1)
        return jnp.concatenate([k, pad, v], 0)

    mine = packed(o)
    other = swap(packed(1 - o), 2)
    qu = trade(jnp.concatenate([quarters(queries), quarters(upstream)], 1))
    pair = jnp.stack([jnp.where(o == 0, mine, other), jnp.where(o == 0, other, mine)])
    k_pair, v_pair = pair[:, :BLK + PAD], pair[:, BLK + PAD:]
    k_line = jnp.stack([k_pair] + [from_z(k_pair, d) for d in (1, 2, 3)])
    v_line = jnp.stack([v_pair] + [from_y(v_pair, d) for d in (1, 2, 3)])
    k_line, v_line = lax.optimization_barrier((k_line, v_line))
    kp = [k_line] + [from_y(k_line, d) for d in (1, 2, 3)]
    vp = [v_line] + [from_z(v_line, d) for d in (1, 2, 3)]
    starts = jnp.sum(total_of([k[:, :, BLK, :8] for k in kp]), (0, 1)).astype(jnp.int32)
    bases = [BLK * (16 * (p >> 1) + 8 * (p & 1) + z % 2 * 4 + y) for p in range(4)]
    scal = jnp.concatenate([starts, jnp.stack(bases + [z, y, member, member]).astype(jnp.int32)])
    w = jnp.broadcast_to(
        lax.dynamic_slice_in_dim(value_weight, member * WIDTH, WIDTH, 0)[:, None], (WIDTH, HD)
    )

    out, lse, critic, qt = forward(scal, qu, kp, vp, w)

    ut, *halved = prepare(scal, qu, kp, vp)
    keys_low, keys_high = halved[0::2], halved[1::2]
    own = (jnp.arange(4)[:, None] == member) & (head == 0)
    critic = lax.psum(critic[:, 0, :] - jnp.where(own, targets[None, :], 0.0), "head")
    err = critic + sum(swap(critic, k) for k in (1, 2, 3))
    value_error = lax.dynamic_index_in_dim(err, member, 0, False)

    part, dout, delta, *grads = upper(scal, qu, ut, qt, *keys_high, w, out, lse, err[:, None, :])
    high = [grads[0]] + [to_y(grads[d], d) for d in (1, 2, 3)]
    dq, *grads = lower(scal, qu, qt, *keys_low, dout, lse, delta, part)
    high, grads = lax.optimization_barrier((high, grads))
    dk_low = [grads[0]] + [to_y(grads[d], d) for d in (1, 2, 3)]
    dv_low = [grads[4]] + [to_z(grads[4 + d], d) for d in (1, 2, 3)]
    dk_low[1], dq = lax.optimization_barrier((dk_low[1], dq))
    high = total_of(high)
    tail = halves(joined(high[2 * LINE:]))
    high = high[:2 * LINE].astype(BF16).reshape(4, 2 * HD, BLK)
    dk_low, dv_low = lax.optimization_barrier((dk_low, dv_low))
    dk_low = total_of(dk_low).astype(BF16).reshape(4, HD, BLK)
    dv_low = total_of(dv_low).astype(BF16).reshape(4, HD, BLK)
    by_z = [jnp.concatenate([dk_low[d], high[d], tail], 0) for d in range(4)]
    by_z = total_of([by_z[0]] + [to_z(by_z[d], d) for d in (1, 2, 3)])
    by_y = total_of([dv_low[0]] + [to_y(dv_low[d], d) for d in (1, 2, 3)])
    readout = joined(by_z[3 * HD:])
    low = jnp.concatenate([by_z[:HD], by_y], 0).astype(BF16)
    high = by_z[HD:3 * HD].astype(BF16)
    mine, other = jnp.where(o == 0, low, high), jnp.where(o == 0, high, low)
    other = swap(jnp.concatenate([other, halves(readout)], 0), 2)
    readout_grad = (readout + joined(other[2 * HD:].astype(F32))).reshape(-1)
    other = other[:2 * HD]
    first, second = jnp.where(o == 0, mine, other), jnp.where(o == 0, other, mine)
    key_grad = jnp.concatenate([first[:HD], second[:HD]], 0).T
    value_grad = jnp.concatenate([first[HD:], second[HD:]], 0).T

    dq = trade(dq)
    query_grad = jnp.concatenate([dq[m] for m in range(4)], 1)
    return (query_grad, key_grad, value_grad, value_error, readout_grad)


def solution(mesh):
    mesh = jax.sharding.Mesh(mesh.devices.reshape(4, 2, 2, 2, 4), ("head", *CTX))
    wide, rows_only = P(CTX, "head"), P(CTX)
    return jax.shard_map(
        local,
        mesh=mesh,
        in_specs=(wide, wide, wide, rows_only, P("head"), rows_only, wide),
        out_specs=(wide, wide, wide, rows_only, P("head")),
        check_vma=False,
    )
```

profile of v0, /device:TPU:0, one launch (start us, length us, event | category | flops | bytes accessed | tf_op | source)
XLA Modules:
  0.0 233.8 jit_solution(7057084783241895381)
XLA Ops:
  0.6 0.8 convert_reduce_fusion
  1.5 1.0 constant_dynamic-slice_fusion.3
  2.6 3.2 %collective-permute-start = (bf16[528,128]{1,0:T(8,128)(2,1)S(1)}, bf16[528,128]{1,0:T(8,128)(2,1)S(1)}, u32[]{:S(2)}, u32[]{:S(2)}) collective-permute-start(bf16[528,128]{1,0:T(8,128)(2,1)S(1)} %fusion.4), channel_id=1, source_target_pairs={{0,16},{1,17},{2,18},{3,19},{4,20},{5,21},{6,22},{7,23},{8,24},{9,... | collective-permute-start | bytes 405512 | tf_op jit(solution)/shard_map/ppermute | solution.py:443
  5.8 1.7 slice_bitcast_fusion.7
  7.5 1.4 maximum_maximum_fusion
  8.9 5.1 %all-to-all-start = ((bf16[4,512,512]{2,1,0:T(8,128)(2,1)}), bf16[4,512,512]{2,1,0:T(8,128)(2,1)}, u32[]{:S(2)}, u32[]{:S(2)}) async-start(bf16[4,512,512]{2,1,0:T(8,128)(2,1)} %maximum_maximum_fusion), calls=%async_computation | async-start | bytes 4194304 | tf_op jit(solution)/shard_map/all_to_all | solution.py:451
  14.2 3.1 %collective-permute-start.4 = (bf16[2,256,128]{2,1,0:T(8,128)(2,1)S(1)}, bf16[2,256,128]{2,1,0:T(8,128)(2,1)S(1)}, u32[]{:S(2)}, u32[]{:S(2)}) collective-permute-start(bf16[2,256,128]{2,1,0:T(8,128)(2,1)S(1)} %pad_maximum_fusion.14), channel_id=1, source_target_pairs={{0,3},{1,0},{2,1},{3,2},{4,7},{5,4},{6,5},{7,6},{8,11},{9,8},{10,9... | collective-permute-start | bytes 393224 | tf_op jit(solution)/shard_map/ppermute | solution.py:443
  17.3 0.7 collective-permute-start.5
  18.0 1.0 collective-permute-start.6
  19.0 3.6 %collective-permute-start.2 = (bf16[2,272,128]{2,1,0:T(8,128)(2,1)S(1)}, bf16[2,272,128]{2,1,0:T(8,128)(2,1)S(1)}, u32[]{:S(2)}, u32[]{:S(2)}) collective-permute-start(bf16[2,272,128]{2,1,0:T(8,128)(2,1)S(1)} %fusion), channel_id=1, source_target_pairs={{0,8},{1,9},{2,10},{3,11},{4,12},{5,13},{6,14},{7,15},{8,0},{9,1},... | collective-permute-start | bytes 417800 | tf_op jit(solution)/shard_map/ppermute | solution.py:443
  22.6 0.4 collective-permute-start.1
  23.0 1.6 collective-permute-start.3
  24.8 1.3 collective-permute-done.6
  26.2 18.6 %collective-permute-done.2 = bf16[2,272,128]{2,1,0:T(8,128)(2,1)S(1)} collective-permute-done((bf16[2,272,128]{2,1,0:T(8,128)(2,1)S(1)}, bf16[2,272,128]{2,1,0:T(8,128)(2,1)S(1)}, u32[]{:S(2)}, u32[]{:S(2)}) %collective-permute-start.2) | collective-permute-done | bytes 139296 | tf_op jit(solution)/shard_map/ppermute | solution.py:443
  44.8 1.4 collective-permute-done.3
  46.4 1.6 collective-permute-start.9
  48.0 2.9 %collective-permute-start.8 = (bf16[4,2,272,128]{3,2,1,0:T(8,128)(2,1)S(1)}, bf16[4,2,272,128]{3,2,1,0:T(8,128)(2,1)S(1)}, u32[]{:S(2)}, u32[]{:S(2)}) collective-permute-start(bf16[4,2,272,128]{3,2,1,0:T(8,128)(2,1)S(1)} %pad_maximum_fusion.1.k0), channel_id=1, source_target_pairs={{0,2},{1,3},{2,0},{3,1},{4,6},{5,7},{6,4},{7,5},{8,10},{9,11},{10,... | collective-permute-start | bytes 1671176 | tf_op jit(solution)/shard_map/ppermute | solution.py:443
  50.9 1.3 collective-permute-start.7
  52.3 1.3 collective-permute-start.12
  53.5 0.9 collective-permute-start.11
  54.4 7.8 %collective-permute-done.9.k3 = bf16[4,2,272,128]{3,2,1,0:T(8,128)(2,1)S(1)} collective-permute-done((bf16[4,2,272,128]{3,2,1,0:T(8,128)(2,1)S(1)}, bf16[4,2,272,128]{3,2,1,0:T(8,128)(2,1)S(1)}, u32[]{:S(2)}, u32[]{:S(2)}) %collective-permute-start.9) | collective-permute-done | bytes 557088 | tf_op jit(solution)/shard_map/ppermute | solution.py:443
  62.3 0.7 collective-permute-start.10
  63.0 0.8 dynamic_slice.23
  63.7 11.6 %collective-permute-done.8.k2 = bf16[4,2,272,128]{3,2,1,0:T(8,128)(2,1)S(1)} collective-permute-done((bf16[4,2,272,128]{3,2,1,0:T(8,128)(2,1)S(1)}, bf16[4,2,272,128]{3,2,1,0:T(8,128)(2,1)S(1)}, u32[]{:S(2)}, u32[]{:S(2)}) %collective-permute-start.8) | collective-permute-done | bytes 557088 | tf_op jit(solution)/shard_map/ppermute | solution.py:443
  75.4 0.8 fusion.12
  76.2 1.6 collective-permute-done.12.v3
  77.8 0.5 collective-permute-done.10.v1
  78.5 18.2 %attention_forward.1 = (bf16[4,4,128,256]{3,2,1,0:T(8,128)(2,1)}, f32[4,4,1,256]{3,2,1,0:T(1,128)S(1)}, f32[4,1,256]{2,1,0:T(1,128)S(1)}, bf16[4,4,128,256]{3,2,1,0:T(8,128)(2,1)}) custom-call(s32[16]{0:T(128)S(1)} %concatenate.54.scal, bf16[4,512,512]{2,1,0:T(8,128)(2,1)} %all-to-all-done.u_ref.q_ref, bf16[4,2,272,128]{3,2,1,0:T(8,128)(2,1)} %copy-done, ...), custom_call_target="tpu_custom_call" | custom-call | flops 8999999488 | bytes 8388608 | tf_op jit(solution)/shard_map/attention_forward/pallas_call | solution.py:372
  96.8 5.6 %psum.7 = f32[4,256]{1,0:T(4,128)S(1)} all-reduce(f32[4,256]{1,0:T(4,128)S(1)} %bitcast_subtract_fusion), channel_id=1, replica_groups=mesh['head'=4,'outer'=2,'zh'=2,'zl'=2,'y'=4] {'head'}, use_global_device_ids=true, to_apply=%region_2.3 | all-reduce | flops 1024 | bytes 8192 | tf_op jit(solution)/shard_map/psum | solution.py:526
  102.4 4.4 %collective-permute-start.15 = (f32[4,256]{1,0:T(4,128)S(1)}, f32[4,256]{1,0:T(4,128)S(1)}, u32[]{:S(2)}, u32[]{:S(2)}) collective-permute-start(f32[4,256]{1,0:T(4,128)S(1)} %psum.7), channel_id=1, source_target_pairs={{0,24},{1,25},{2,26},{3,27},{4,28},{5,29},{6,30},{7,31},{8,16},{9,... | collective-permute-start | bytes 12296 | tf_op jit(solution)/shard_map/ppermute | solution.py:443
  106.8 0.2 collective-permute-start.14
  107.0 2.0 collective-permute-start.13
  109.0 6.4 %prepare_backward.1 = (bf16[4,4,128,256]{3,2,1,0:T(8,128)(2,1)}, bf16[4096,128]{1,0:T(8,128)(2,1)}, bf16[4096,128]{1,0:T(8,128)(2,1)}, bf16[16,128,256]{2,1,0:T(...) custom-call(s32[16]{0:T(128)S(1)} %concatenate.54.scal, ...), custom_call_target="tpu_custom_call" | custom-call | flops 100000000 | bytes 8388608 | tf_op jit(solution)/shard_map/prepare_backward/pallas_call | solution.py:372
  115.4 14.2 %attention_upper.1 = (bf16[4,4,256,128]{3,2,1,0:T(8,128)(2,1)}, bf16[4,4,128,256]{3,2,1,0:T(8,128)(2,1)}, f32[4,4,1,256]{3,2,1,0:T(1,128)S(1)}, bf16[1040,256]{1...) custom-call(s32[16]{0:T(128)S(1)} %concatenate.54.scal, ...), custom_call_target="tpu_custom_call" | custom-call | flops 8000000000 | bytes 8388608 | tf_op jit(solution)/shard_map/attention_upper/pallas_call | solution.py:372
  129.6 4.9 %collective-permute-start.16 = (bf16[1040,256]{1,0:T(8,128)(2,1)S(1)}, bf16[1040,256]{1,0:T(8,128)(2,1)S(1)}, u32[]{:S(2)}, u32[]{:S(2)}) collective-permute-start(bf16[1040,256]{1,0:T(8,128)(2,1)S(1)} %get-tuple-element.67), channel_id=1, source_target_pairs={{0,1},{1,2},{2,3},{3,0},{4,5},{5,6},{6,7},{7,4},{8,9},{9,10},{10,1... | collective-permute-start | bytes 1597448 | tf_op jit(solution)/shard_map/ppermute | solution.py:443
  134.5 9.8 %collective-permute-start.17 = (bf16[1040,256]{1,0:T(8,128)(2,1)S(1)}, bf16[1040,256]{1,0:T(8,128)(2,1)S(1)}, u32[]{:S(2)}, u32[]{:S(2)}) collective-permute-start(bf16[1040,256]{1,0:T(8,128)(2,1)S(1)} %get-tuple-element.68), channel_id=1, source_target_pairs={{0,2},{1,3},{2,0},{3,1},{4,6},{5,7},{6,4},{7,5},{8,10},{9,11},{10,... | collective-permute-start | bytes 1597448 | tf_op jit(solution)/shard_map/ppermute | solution.py:443
  144.4 2.5 %collective-permute-start.18 = (bf16[1040,256]{1,0:T(8,128)(2,1)}, bf16[1040,256]{1,0:T(8,128)(2,1)S(1)}, u32[]{:S(2)}, u32[]{:S(2)}) collective-permute-start(bf16[1040,256]{1,0:T(8,128)(2,1)} %get-tuple-element.69), channel_id=1, source_target_pairs={{0,3},{1,0},{2,1},{3,2},{4,7},{5,4},{6,5},{7,6},{8,11},{9,8},{10,9... | collective-permute-start | bytes 1597448 | tf_op jit(solution)/shard_map/ppermute | solution.py:443
  146.9 17.6 %attention_lower.1 = (bf16[4,256,512]{2,1,0:T(8,128)(2,1)}, bf16[512,256]{1,0:T(8,128)(2,1)S(1)}, bf16[512,256]{1,0:T(8,128)(2,1)S(1)}, bf16[512,256]{1,0:T(8,12...) custom-call(s32[16]{0:T(128)S(1)} %concatenate.54.scal, ...), custom_call_target="tpu_custom_call" | custom-call | flops 16000000000 | bytes 8388608 | tf_op jit(solution)/shard_map/attention_lower/pallas_call | solution.py:372
  164.5 2.4 %collective-permute-done.17 = bf16[1040,256]{1,0:T(8,128)(2,1)S(1)} collective-permute-done((bf16[1040,256]{1,0:T(8,128)(2,1)S(1)}, bf16[1040,256]{1,0:T(8,128)(2,1)S(1)}, u32[]{:S(2)}, u32[]{:S(2)}) %collective-permute-start.17) | collective-permute-done | bytes 532512 | tf_op jit(solution)/shard_map/ppermute | solution.py:443
  167.0 1.6 collective-permute-start.19
  168.6 2.2 collective-permute-start.20
  170.8 2.4 %collective-permute-start.21 = (bf16[512,256]{1,0:T(8,128)(2,1)S(1)}, bf16[512,256]{1,0:T(8,128)(2,1)S(1)}, u32[]{:S(2)}, u32[]{:S(2)}) collective-permute-start(bf16[512,256]{1,0:T(8,128)(2,1)S(1)} %get-tuple-element.90), channel_id=1, source_target_pairs={{0,3},{1,0},{2,1},{3,2},{4,7},{5,4},{6,5},{7,6},{8,11},{9,8},{10,9... | collective-permute-start | bytes 786440 | tf_op jit(solution)/shard_map/ppermute | solution.py:443
  173.2 13.3 %collective-permute-start.22 = (bf16[512,256]{1,0:T(8,128)(2,1)S(1)}, bf16[512,256]{1,0:T(8,128)(2,1)S(1)}, u32[]{:S(2)}, u32[]{:S(2)}) collective-permute-start(bf16[512,256]{1,0:T(8,128)(2,1)S(1)} %get-tuple-element.92), channel_id=1, source_target_pairs={{0,4},{1,5},{2,6},{3,7},{4,8},{5,9},{6,10},{7,11},{8,12},{9,13},{1... | collective-permute-start | bytes 786440 | tf_op jit(solution)/shard_map/ppermute | solution.py:443
  186.5 2.1 collective-permute-start.23
  188.6 0.3 fusion.16
  188.9 1.5 collective-permute-start.24
  190.5 3.5 %collective-permute-done.22 = bf16[512,256]{1,0:T(8,128)(2,1)S(1)} collective-permute-done((bf16[512,256]{1,0:T(8,128)(2,1)S(1)}, bf16[512,256]{1,0:T(8,128)(2,1)S(1)}, u32[]{:S(2)}, u32[]{:S(2)}) %collective-permute-start.22) | collective-permute-done | bytes 262176 | tf_op jit(solution)/shard_map/ppermute | solution.py:443
  194.0 4.0 %collective-permute-done.23 = bf16[512,256]{1,0:T(8,128)(2,1)S(1)} collective-permute-done((bf16[512,256]{1,0:T(8,128)(2,1)S(1)}, bf16[512,256]{1,0:T(8,128)(2,1)S(1)}, u32[]{:S(2)}, u32[]{:S(2)}) %collective-permute-start.23) | collective-permute-done | bytes 262176 | tf_op jit(solution)/shard_map/ppermute | solution.py:443
  198.4 1.1 collective-permute-start.28
  199.5 2.2 collective-permute-start.30
  201.7 1.4 collective-permute-start.29
  203.2 1.9 collective-permute-start.25
  205.1 3.3 %collective-permute-start.26 = (bf16[400,256]{1,0:T(8,128)(2,1)S(1)}, bf16[400,256]{1,0:T(8,128)(2,1)S(1)}, u32[]{:S(2)}, u32[]{:S(2)}) collective-permute-start(bf16[400,256]{1,0:T(8,128)(2,1)S(1)} %get-tuple-element.161), channel_id=1, source_target_pairs={{0,8},{1,9},{2,10},{3,11},{4,12},{5,13},{6,14},{7,15},{8,0},{9,1},... | collective-permute-start | bytes 614408 | tf_op jit(solution)/shard_map/ppermute | solution.py:443
  208.5 2.2 collective-permute-done.25
  210.7 3.7 %collective-permute-done.26 = bf16[400,256]{1,0:T(8,128)(2,1)S(1)} collective-permute-done((bf16[400,256]{1,0:T(8,128)(2,1)S(1)}, bf16[400,256]{1,0:T(8,128)(2,1)S(1)}, u32[]{:S(2)}, u32[]{:S(2)}) %collective-permute-start.26) | collective-permute-done | bytes 204832 | tf_op jit(solution)/shard_map/ppermute | solution.py:443
  214.6 3.2 %collective-permute-start.31 = (bf16[272,256]{1,0:T(8,128)(2,1)S(1)}, bf16[272,256]{1,0:T(8,128)(2,1)S(1)}, u32[]{:S(2)}, u32[]{:S(2)}) collective-permute-start(bf16[272,256]{1,0:T(8,128)(2,1)S(1)} %pad_maximum_fusion.13), channel_id=1, source_target_pairs={{0,16},{1,17},{2,18},{3,19},{4,20},{5,21},{6,22},{7,23},{8,24},{9,... | collective-permute-start | bytes 417800 | tf_op jit(solution)/shard_map/ppermute | solution.py:443
  217.7 0.6 constant_dynamic-slice_fusion
  218.3 3.5 %all-to-all-start.1 = ((bf16[4,256,512]{2,1,0:T(8,128)(2,1)}), bf16[4,256,512]{2,1,0:T(8,128)(2,1)S(1)}, u32[]{:S(2)}, u32[]{:S(2)}) async-start(bf16[4,256,512]{2,1,0:T(8,128)(2,1)} %get-tuple-element.86), calls=%async_computation.1 | async-start | bytes 2097152 | tf_op jit(solution)/shard_map/all_to_all | solution.py:451
  221.8 0.9 collective-permute-done.31
  222.8 0.6 copy.17
  223.4 0.8 copy.15
  224.2 0.8 copy.14
  225.0 7.7 %all-to-all-done.1 = bf16[4,256,512]{2,1,0:T(8,128)(2,1)S(1)} async-done(((bf16[4,256,512]{2,1,0:T(8,128)(2,1)}), bf16[4,256,512]{2,1,0:T(8,128)(2,1)S(1)}, u32[]{:S(2)}, u32[]{:S(2)}) %all-to-all-start.1) | async-done | bytes 1048608 | tf_op jit(solution)/shard_map/all_to_all | solution.py:451
  232.7 1.1 pad_maximum_fusion
  (70 shorter events, 1.9 us)
Async XLA Ops:
  2.6 11.4 %collective-permute-start = (bf16[528,128]{1,0:T(8,128)(2,1)S(1)}, bf16[528,128]{1,0:T(8,128)(2,1)S(1)}, u32[]{:S(2)}, u32[]{:S(2)}) collective-permute-start(bf16[528,128]{1,0:T(8,128)(2,1)S(1)} %fusion.4), channel_id=1, source_target_pairs={{0,16},{1,17},{2,18},{3,19},{4,20},{5,21},{6,22},{7,23},{8,24},{9,... | collective-permute-start | bytes 405512 | tf_op jit(solution)/shard_map/ppermute | solution.py:443
  8.9 69.4 %all-to-all-start = ((bf16[4,512,512]{2,1,0:T(8,128)(2,1)}), bf16[4,512,512]{2,1,0:T(8,128)(2,1)}, u32[]{:S(2)}, u32[]{:S(2)}) async-start(bf16[4,512,512]{2,1,0:T(8,128)(2,1)} %maximum_maximum_fusion), calls=%async_computation | async-start | bytes 4194304 | tf_op jit(solution)/shard_map/all_to_all | solution.py:451
  14.2 8.8 %collective-permute-start.4 = (bf16[2,256,128]{2,1,0:T(8,128)(2,1)S(1)}, bf16[2,256,128]{2,1,0:T(8,128)(2,1)S(1)}, u32[]{:S(2)}, u32[]{:S(2)}) collective-permute-start(bf16[2,256,128]{2,1,0:T(8,128)(2,1)S(1)} %pad_maximum_fusion.14), channel_id=1, source_target_pairs={{0,3},{1,0},{2,1},{3,2},{4,7},{5,4},{6,5},{7,6},{8,11},{9,8},{10,9... | collective-permute-start | bytes 393224 | tf_op jit(solution)/shard_map/ppermute | solution.py:443
  17.3 7.4 %collective-permute-start.5 = (bf16[2,256,128]{2,1,0:T(8,128)(2,1)S(1)}, bf16[2,256,128]{2,1,0:T(8,128)(2,1)S(1)}, u32[]{:S(2)}, u32[]{:S(2)}) collective-permute-start(bf16[2,256,128]{2,1,0:T(8,128)(2,1)S(1)} %pad_maximum_fusion.14), channel_id=1, source_target_pairs={{0,2},{1,3},{2,0},{3,1},{4,6},{5,7},{6,4},{7,5},{8,10},{9,11},{10,... | collective-permute-start | bytes 393224 | tf_op jit(solution)/shard_map/ppermute | solution.py:443
  18.0 8.1 %collective-permute-start.6 = (bf16[2,256,128]{2,1,0:T(8,128)(2,1)S(1)}, bf16[2,256,128]{2,1,0:T(8,128)(2,1)S(1)}, u32[]{:S(2)}, u32[]{:S(2)}) collective-permute-start(bf16[2,256,128]{2,1,0:T(8,128)(2,1)S(1)} %pad_maximum_fusion.14), channel_id=1, source_target_pairs={{0,1},{1,2},{2,3},{3,0},{4,5},{5,6},{6,7},{7,4},{8,9},{9,10},{10,1... | collective-permute-start | bytes 393224 | tf_op jit(solution)/shard_map/ppermute | solution.py:443
  19.0 25.8 %collective-permute-start.2 = (bf16[2,272,128]{2,1,0:T(8,128)(2,1)S(1)}, bf16[2,272,128]{2,1,0:T(8,128)(2,1)S(1)}, u32[]{:S(2)}, u32[]{:S(2)}) collective-permute-start(bf16[2,272,128]{2,1,0:T(8,128)(2,1)S(1)} %fusion), channel_id=1, source_target_pairs={{0,8},{1,9},{2,10},{3,11},{4,12},{5,13},{6,14},{7,15},{8,0},{9,1},... | collective-permute-start | bytes 417800 | tf_op jit(solution)/shard_map/ppermute | solution.py:443
  22.6 22.2 %collective-permute-start.1 = (bf16[2,272,128]{2,1,0:T(8,128)(2,1)S(1)}, bf16[2,272,128]{2,1,0:T(8,128)(2,1)S(1)}, u32[]{:S(2)}, u32[]{:S(2)}) collective-permute-start(bf16[2,272,128]{2,1,0:T(8,128)(2,1)S(1)} %fusion), channel_id=1, source_target_pairs={{0,12},{1,13},{2,14},{3,15},{4,0},{5,1},{6,2},{7,3},{8,4},{9,5},{1... | collective-permute-start | bytes 417800 | tf_op jit(solution)/shard_map/ppermute | solution.py:443
  23.0 23.2 %collective-permute-start.3 = (bf16[2,272,128]{2,1,0:T(8,128)(2,1)S(1)}, bf16[2,272,128]{2,1,0:T(8,128)(2,1)S(1)}, u32[]{:S(2)}, u32[]{:S(2)}) collective-permute-start(bf16[2,272,128]{2,1,0:T(8,128)(2,1)S(1)} %fusion), channel_id=1, source_target_pairs={{0,4},{1,5},{2,6},{3,7},{4,8},{5,9},{6,10},{7,11},{8,12},{9,13},{1... | collective-permute-start | bytes 417800 | tf_op jit(solution)/shard_map/ppermute | solution.py:443
  46.4 32.1 %copy-start = (bf16[4,2,272,128]{3,2,1,0:T(8,128)(2,1)}, bf16[4,2,272,128]{3,2,1,0:T(8,128)(2,1)S(1)}, u32[]{:S(2)}) copy-start(bf16[4,2,272,128]{3,2,1,0:T(8,128)(2,1)S(1)} %pad_maximum_fusion.1.k0) | copy-start | bytes 1671172
  46.4 15.9 %collective-permute-start.9 = (bf16[4,2,272,128]{3,2,1,0:T(8,128)(2,1)S(1)}, bf16[4,2,272,128]{3,2,1,0:T(8,128)(2,1)S(1)}, u32[]{:S(2)}, u32[]{:S(2)}) collective-permute-start(bf16[4,2,272,128]{3,2,1,0:T(8,128)(2,1)S(1)} %pad_maximum_fusion.1.k0), channel_id=1, source_target_pairs={{0,1},{1,2},{2,3},{3,0},{4,5},{5,6},{6,7},{7,4},{8,9},{9,10},{10,1... | collective-permute-start | bytes 1671176 | tf_op jit(solution)/shard_map/ppermute | solution.py:443
  48.0 27.4 %collective-permute-start.8 = (bf16[4,2,272,128]{3,2,1,0:T(8,128)(2,1)S(1)}, bf16[4,2,272,128]{3,2,1,0:T(8,128)(2,1)S(1)}, u32[]{:S(2)}, u32[]{:S(2)}) collective-permute-start(bf16[4,2,272,128]{3,2,1,0:T(8,128)(2,1)S(1)} %pad_maximum_fusion.1.k0), channel_id=1, source_target_pairs={{0,2},{1,3},{2,0},{3,1},{4,6},{5,7},{6,4},{7,5},{8,10},{9,11},{10,... | collective-permute-start | bytes 1671176 | tf_op jit(solution)/shard_map/ppermute | solution.py:443
  50.9 24.5 %collective-permute-start.7 = (bf16[4,2,272,128]{3,2,1,0:T(8,128)(2,1)S(1)}, bf16[4,2,272,128]{3,2,1,0:T(8,128)(2,1)}, u32[]{:S(2)}, u32[]{:S(2)}) collective-permute-start(bf16[4,2,272,128]{3,2,1,0:T(8,128)(2,1)S(1)} %pad_maximum_fusion.1.k0), channel_id=1, source_target_pairs={{0,3},{1,0},{2,1},{3,2},{4,7},{5,4},{6,5},{7,6},{8,11},{9,8},{10,9... | collective-permute-start | bytes 1671176 | tf_op jit(solution)/shard_map/ppermute | solution.py:443
  52.3 25.6 %collective-permute-start.12 = (bf16[4,2,256,128]{3,2,1,0:T(8,128)(2,1)S(1)}, bf16[4,2,256,128]{3,2,1,0:T(8,128)(2,1)}, u32[]{:S(2)}, u32[]{:S(2)}) collective-permute-start(bf16[4,2,256,128]{3,2,1,0:T(8,128)(2,1)S(1)} %pad_maximum_fusion.2.v0), channel_id=1, source_target_pairs={{0,4},{1,5},{2,6},{3,7},{4,8},{5,9},{6,10},{7,11},{8,12},{9,13},{1... | collective-permute-start | bytes 1572872 | tf_op jit(solution)/shard_map/ppermute | solution.py:443
  53.5 24.3 %collective-permute-start.11 = (bf16[4,2,256,128]{3,2,1,0:T(8,128)(2,1)S(1)}, bf16[4,2,256,128]{3,2,1,0:T(8,128)(2,1)S(1)}, u32[]{:S(2)}, u32[]{:S(2)}) collective-permute-start(bf16[4,2,256,128]{3,2,1,0:T(8,128)(2,1)S(1)} %pad_maximum_fusion.2.v0), channel_id=1, source_target_pairs={{0,8},{1,9},{2,10},{3,11},{4,12},{5,13},{6,14},{7,15},{8,0},{9,1},... | collective-permute-start | bytes 1572872 | tf_op jit(solution)/shard_map/ppermute | solution.py:443
  62.3 16.2 %copy-start.1 = (bf16[4,2,272,128]{3,2,1,0:T(8,128)(2,1)}, bf16[4,2,272,128]{3,2,1,0:T(8,128)(2,1)S(1)}, u32[]{:S(2)}) copy-start(bf16[4,2,272,128]{3,2,1,0:T(8,128)(2,1)S(1)} %collective-permute-done.9.k3) | copy-start | bytes 1671172
  62.3 16.0 %collective-permute-start.10 = (bf16[4,2,256,128]{3,2,1,0:T(8,128)(2,1)S(1)}, bf16[4,2,256,128]{3,2,1,0:T(8,128)(2,1)S(1)}, u32[]{:S(2)}, u32[]{:S(2)}) collective-permute-start(bf16[4,2,256,128]{3,2,1,0:T(8,128)(2,1)S(1)} %pad_maximum_fusion.2.v0), channel_id=1, source_target_pairs={{0,12},{1,13},{2,14},{3,15},{4,0},{5,1},{6,2},{7,3},{8,4},{9,5},{1... | collective-permute-start | bytes 1572872 | tf_op jit(solution)/shard_map/ppermute | solution.py:443
  75.4 3.1 %copy-start.2 = (bf16[4,2,272,128]{3,2,1,0:T(8,128)(2,1)}, bf16[4,2,272,128]{3,2,1,0:T(8,128)(2,1)S(1)}, u32[]{:S(2)}) copy-start(bf16[4,2,272,128]{3,2,1,0:T(8,128)(2,1)S(1)} %collective-permute-done.8.k2) | copy-start | bytes 1671172
  78.5 18.3 %copy-start.3 = (f32[256]{0:T(256)S(1)}, f32[256]{0:T(256)}, u32[]{:S(2)}) copy-start(f32[256]{0:T(256)} %param.12) | copy-start | bytes 3076
  102.4 13.0 %collective-permute-start.15 = (f32[4,256]{1,0:T(4,128)S(1)}, f32[4,256]{1,0:T(4,128)S(1)}, u32[]{:S(2)}, u32[]{:S(2)}) collective-permute-start(f32[4,256]{1,0:T(4,128)S(1)} %psum.7), channel_id=1, source_target_pairs={{0,24},{1,25},{2,26},{3,27},{4,28},{5,29},{6,30},{7,31},{8,16},{9,... | collective-permute-start | bytes 12296 | tf_op jit(solution)/shard_map/ppermute | solution.py:443
  106.8 8.6 %collective-permute-start.14 = (f32[4,256]{1,0:T(4,128)S(1)}, f32[4,256]{1,0:T(4,128)S(1)}, u32[]{:S(2)}, u32[]{:S(2)}) collective-permute-start(f32[4,256]{1,0:T(4,128)S(1)} %psum.7), channel_id=1, source_target_pairs={{0,16},{1,17},{2,18},{3,19},{4,20},{5,21},{6,22},{7,23},{8,24},{9,... | collective-permute-start | bytes 12296 | tf_op jit(solution)/shard_map/ppermute | solution.py:443
  107.0 8.4 %collective-permute-start.13 = (f32[4,256]{1,0:T(4,128)S(1)}, f32[4,256]{1,0:T(4,128)S(1)}, u32[]{:S(2)}, u32[]{:S(2)}) collective-permute-start(f32[4,256]{1,0:T(4,128)S(1)} %psum.7), channel_id=1, source_target_pairs={{0,8},{1,9},{2,10},{3,11},{4,12},{5,13},{6,14},{7,15},{8,0},{9,1},... | collective-permute-start | bytes 12296 | tf_op jit(solution)/shard_map/ppermute | solution.py:443
  129.6 34.9 %collective-permute-start.16 = (bf16[1040,256]{1,0:T(8,128)(2,1)S(1)}, bf16[1040,256]{1,0:T(8,128)(2,1)S(1)}, u32[]{:S(2)}, u32[]{:S(2)}) collective-permute-start(bf16[1040,256]{1,0:T(8,128)(2,1)S(1)} %get-tuple-element.67), channel_id=1, source_target_pairs={{0,1},{1,2},{2,3},{3,0},{4,5},{5,6},{6,7},{7,4},{8,9},{9,10},{10,1... | collective-permute-start | bytes 1597448 | tf_op jit(solution)/shard_map/ppermute | solution.py:443
  134.5 32.4 %collective-permute-start.17 = (bf16[1040,256]{1,0:T(8,128)(2,1)S(1)}, bf16[1040,256]{1,0:T(8,128)(2,1)S(1)}, u32[]{:S(2)}, u32[]{:S(2)}) collective-permute-start(bf16[1040,256]{1,0:T(8,128)(2,1)S(1)} %get-tuple-element.68), channel_id=1, source_target_pairs={{0,2},{1,3},{2,0},{3,1},{4,6},{5,7},{6,4},{7,5},{8,10},{9,11},{10,... | collective-permute-start | bytes 1597448 | tf_op jit(solution)/shard_map/ppermute | solution.py:443
  144.4 22.6 %collective-permute-start.18 = (bf16[1040,256]{1,0:T(8,128)(2,1)}, bf16[1040,256]{1,0:T(8,128)(2,1)S(1)}, u32[]{:S(2)}, u32[]{:S(2)}) collective-permute-start(bf16[1040,256]{1,0:T(8,128)(2,1)} %get-tuple-element.69), channel_id=1, source_target_pairs={{0,3},{1,0},{2,1},{3,2},{4,7},{5,4},{6,5},{7,6},{8,11},{9,8},{10,9... | collective-permute-start | bytes 1597448 | tf_op jit(solution)/shard_map/ppermute | solution.py:443
  164.5 24.4 %copy-start.4 = (bf16[512,256]{1,0:T(8,128)(2,1)S(1)}, bf16[512,256]{1,0:T(8,128)(2,1)}, u32[]{:S(2)}) copy-start(bf16[512,256]{1,0:T(8,128)(2,1)} %get-tuple-element.94) | copy-start | bytes 786436
  167.0 21.9 %collective-permute-start.19 = (bf16[512,256]{1,0:T(8,128)(2,1)S(1)}, bf16[512,256]{1,0:T(8,128)(2,1)S(1)}, u32[]{:S(2)}, u32[]{:S(2)}) collective-permute-start(bf16[512,256]{1,0:T(8,128)(2,1)S(1)} %get-tuple-element.84), channel_id=1, source_target_pairs={{0,1},{1,2},{2,3},{3,0},{4,5},{5,6},{6,7},{7,4},{8,9},{9,10},{10,1... | collective-permute-start | bytes 786440 | tf_op jit(solution)/shard_map/ppermute | solution.py:443
  168.6 21.8 %collective-permute-start.20 = (bf16[512,256]{1,0:T(8,128)(2,1)S(1)}, bf16[512,256]{1,0:T(8,128)(2,1)S(1)}, u32[]{:S(2)}, u32[]{:S(2)}) collective-permute-start(bf16[512,256]{1,0:T(8,128)(2,1)S(1)} %get-tuple-element.89), channel_id=1, source_target_pairs={{0,2},{1,3},{2,0},{3,1},{4,6},{5,7},{6,4},{7,5},{8,10},{9,11},{10,... | collective-permute-start | bytes 786440 | tf_op jit(solution)/shard_map/ppermute | solution.py:443
  170.8 19.7 %collective-permute-start.21 = (bf16[512,256]{1,0:T(8,128)(2,1)S(1)}, bf16[512,256]{1,0:T(8,128)(2,1)S(1)}, u32[]{:S(2)}, u32[]{:S(2)}) collective-permute-start(bf16[512,256]{1,0:T(8,128)(2,1)S(1)} %get-tuple-element.90), channel_id=1, source_target_pairs={{0,3},{1,0},{2,1},{3,2},{4,7},{5,4},{6,5},{7,6},{8,11},{9,8},{10,9... | collective-permute-start | bytes 786440 | tf_op jit(solution)/shard_map/ppermute | solution.py:443
  173.2 20.8 %collective-permute-start.22 = (bf16[512,256]{1,0:T(8,128)(2,1)S(1)}, bf16[512,256]{1,0:T(8,128)(2,1)S(1)}, u32[]{:S(2)}, u32[]{:S(2)}) collective-permute-start(bf16[512,256]{1,0:T(8,128)(2,1)S(1)} %get-tuple-element.92), channel_id=1, source_target_pairs={{0,4},{1,5},{2,6},{3,7},{4,8},{5,9},{6,10},{7,11},{8,12},{9,13},{1... | collective-permute-start | bytes 786440 | tf_op jit(solution)/shard_map/ppermute | solution.py:443
  186.5 11.5 %collective-permute-start.23 = (bf16[512,256]{1,0:T(8,128)(2,1)S(1)}, bf16[512,256]{1,0:T(8,128)(2,1)S(1)}, u32[]{:S(2)}, u32[]{:S(2)}) collective-permute-start(bf16[512,256]{1,0:T(8,128)(2,1)S(1)} %get-tuple-element.93), channel_id=1, source_target_pairs={{0,8},{1,9},{2,10},{3,11},{4,12},{5,13},{6,14},{7,15},{8,0},{9,1},... | collective-permute-start | bytes 786440 | tf_op jit(solution)/shard_map/ppermute | solution.py:443
  188.9 9.1 %collective-permute-start.24 = (bf16[512,256]{1,0:T(8,128)(2,1)S(1)}, bf16[512,256]{1,0:T(8,128)(2,1)S(1)}, u32[]{:S(2)}, u32[]{:S(2)}) collective-permute-start(bf16[512,256]{1,0:T(8,128)(2,1)S(1)} %copy-done.4), channel_id=1, source_target_pairs={{0,12},{1,13},{2,14},{3,15},{4,0},{5,1},{6,2},{7,3},{8,4},{9,5},{1... | collective-permute-start | bytes 786440 | tf_op jit(solution)/shard_map/ppermute | solution.py:443
  198.4 10.0 %collective-permute-start.28 = (bf16[128,256]{1,0:T(8,128)(2,1)S(1)}, bf16[128,256]{1,0:T(8,128)(2,1)S(1)}, u32[]{:S(2)}, u32[]{:S(2)}) collective-permute-start(bf16[128,256]{1,0:T(8,128)(2,1)S(1)} %get-tuple-element.145), channel_id=1, source_target_pairs={{0,1},{1,2},{2,3},{3,0},{4,5},{5,6},{6,7},{7,4},{8,9},{9,10},{10,1... | collective-permute-start | bytes 196616 | tf_op jit(solution)/shard_map/ppermute | solution.py:443
  199.5 8.9 %collective-permute-start.30 = (bf16[128,256]{1,0:T(8,128)(2,1)S(1)}, bf16[128,256]{1,0:T(8,128)(2,1)S(1)}, u32[]{:S(2)}, u32[]{:S(2)}) collective-permute-start(bf16[128,256]{1,0:T(8,128)(2,1)S(1)} %get-tuple-element.146), channel_id=1, source_target_pairs={{0,3},{1,0},{2,1},{3,2},{4,7},{5,4},{6,5},{7,6},{8,11},{9,8},{10,9... | collective-permute-start | bytes 196616 | tf_op jit(solution)/shard_map/ppermute | solution.py:443
  201.7 6.7 %collective-permute-start.29 = (bf16[128,256]{1,0:T(8,128)(2,1)S(1)}, bf16[128,256]{1,0:T(8,128)(2,1)S(1)}, u32[]{:S(2)}, u32[]{:S(2)}) collective-permute-start(bf16[128,256]{1,0:T(8,128)(2,1)S(1)} %get-tuple-element.147), channel_id=1, source_target_pairs={{0,2},{1,3},{2,0},{3,1},{4,6},{5,7},{6,4},{7,5},{8,10},{9,11},{10,... | collective-permute-start | bytes 196616 | tf_op jit(solution)/shard_map/ppermute | solution.py:443
  203.2 7.5 %collective-permute-start.25 = (bf16[400,256]{1,0:T(8,128)(2,1)S(1)}, bf16[400,256]{1,0:T(8,128)(2,1)S(1)}, u32[]{:S(2)}, u32[]{:S(2)}) collective-permute-start(bf16[400,256]{1,0:T(8,128)(2,1)S(1)} %get-tuple-element.160), channel_id=1, source_target_pairs={{0,4},{1,5},{2,6},{3,7},{4,8},{5,9},{6,10},{7,11},{8,12},{9,13},{1... | collective-permute-start | bytes 614408 | tf_op jit(solution)/shard_map/ppermute | solution.py:443
  205.1 9.2 %collective-permute-start.26 = (bf16[400,256]{1,0:T(8,128)(2,1)S(1)}, bf16[400,256]{1,0:T(8,128)(2,1)S(1)}, u32[]{:S(2)}, u32[]{:S(2)}) collective-permute-start(bf16[400,256]{1,0:T(8,128)(2,1)S(1)} %get-tuple-element.161), channel_id=1, source_target_pairs={{0,8},{1,9},{2,10},{3,11},{4,12},{5,13},{6,14},{7,15},{8,0},{9,1},... | collective-permute-start | bytes 614408 | tf_op jit(solution)/shard_map/ppermute | solution.py:443
  208.4 5.9 %collective-permute-start.27 = (bf16[400,256]{1,0:T(8,128)(2,1)S(1)}, bf16[400,256]{1,0:T(8,128)(2,1)S(1)}, u32[]{:S(2)}, u32[]{:S(2)}) collective-permute-start(bf16[400,256]{1,0:T(8,128)(2,1)S(1)} %get-tuple-element.162), channel_id=1, source_target_pairs={{0,12},{1,13},{2,14},{3,15},{4,0},{5,1},{6,2},{7,3},{8,4},{9,5},{1... | collective-permute-start | bytes 614408 | tf_op jit(solution)/shard_map/ppermute | solution.py:443
  214.6 8.1 %collective-permute-start.31 = (bf16[272,256]{1,0:T(8,128)(2,1)S(1)}, bf16[272,256]{1,0:T(8,128)(2,1)S(1)}, u32[]{:S(2)}, u32[]{:S(2)}) collective-permute-start(bf16[272,256]{1,0:T(8,128)(2,1)S(1)} %pad_maximum_fusion.13), channel_id=1, source_target_pairs={{0,16},{1,17},{2,18},{3,19},{4,20},{5,21},{6,22},{7,23},{8,24},{9,... | collective-permute-start | bytes 417800 | tf_op jit(solution)/shard_map/ppermute | solution.py:443
  218.3 14.4 %all-to-all-start.1 = ((bf16[4,256,512]{2,1,0:T(8,128)(2,1)}), bf16[4,256,512]{2,1,0:T(8,128)(2,1)S(1)}, u32[]{:S(2)}, u32[]{:S(2)}) async-start(bf16[4,256,512]{2,1,0:T(8,128)(2,1)} %get-tuple-element.86), calls=%async_computation.1 | async-start | bytes 2097152 | tf_op jit(solution)/shard_map/all_to_all | solution.py:451
where the time goes:
time: 233 us; the launch traced here: 234 us
  starting transfers between devices  91.1 us (39%)
  waiting for transfers between devices  67.5 us (29%)
  Pallas kernels  56.4 us (24%)
  local copies, waits for them, and re-layouts  6.53 us (3%)
  other arithmetic  5.64 us (2%)
  blocking collectives  5.63 us (2%)
    ppermute x32, starting transfers between devices, send(): return lax.ppermute(x, CTX, pairs)  82.4 us
    ppermute x32, waiting for transfers between devices, send(): return lax.ppermute(x, CTX, pairs)  59.8 us
    pallas_call x4, Pallas kernels, call(): pl.pallas_call(kernel, grid=(4 if split else 1,), out_shape=tuple(shapes)...  56.4 us
    all_to_all x2, starting transfers between devices, trade(): return lax.all_to_all(x, GROUP, 0, 0, tiled=True)  8.66 us
    all_to_all x2, waiting for transfers between devices, trade(): return lax.all_to_all(x, GROUP, 0, 0, tiled=True)  7.71 us
    psum x1, blocking collectives, local(): lax.psum(critic[:, 0, :] - jnp.where(own, targets[None, :], 0.0), 'head')  5.63 us
  transfers between devices with their start and end apart: 34, of which 15 were waited for; matrix products, arithmetic and copies ran while one was open for 4% of the time, Pallas kernels for 10%

commit v1 on v0

--- a/solution.py
+++ b/solution.py
@@ -45,12 +45,14 @@
     return 16 * o + 4 * z + y
 
 
-def place(scal, pieces, z_first, put):
+def place(scal, main, rest, put_k, put_v):
     for far in range(4):
         for near in range(4):
-            for o in range(2):
-                dz, dy = (near, far) if z_first else (far, near)
-                put(block_of(scal, 0, dz, dy), o, pieces[far][near, o, :BLK, :])
+            b = block_of(scal, 0, near, far)
+            put_k(b, 0, main[far][near, :BLK, :])
+            put_k(b, 1, main[far][near, BLK + PAD:2 * BLK + PAD, :])
+            put_v(b, 0, main[far][near, 2 * (BLK + PAD):, :])
+            put_v(block_of(scal, 0, far, near), 1, rest[far][near])
 
 
 def start_of(scal, pos):
@@ -87,14 +89,18 @@
         body(full + tile * t, tile, False)
         return c
 
-    def single(kb, c):
-        body(kb, 1, False)
-        return c
-
     count = (stop - full) // tile
     lax.fori_loop(first, full, masked, 0)
     lax.fori_loop(0, count, plain, 0)
-    lax.fori_loop(full + tile * count, stop, single, 0)
+    rest = full + tile * count
+
+    @pl.when(stop - rest >= 2)
+    def _():
+        body(rest, 2, False)
+
+    @pl.when((stop - rest) % 2 == 1)
+    def _():
+        body(stop - 1, 1, False)
 
 
 def largest_norm(blocks):
@@ -130,8 +136,7 @@
         def put_v(b, o, blk):
             vt_all[b + 16 * o] = blk.T
 
-        place(scal, (k0, k1, k2, k3), True, put_k)
-        place(scal, (v0, v1, v2, v3), False, put_v)
+        place(scal, (k0, k1, k2, k3), (v0, v1, v2, v3), put_k, put_v)
         small = query_norm * largest_norm(norms) * SCALE2 * SCALE2 <= 3600.0
         flag[0] = small.astype(jnp.int32)
 
@@ -216,8 +221,7 @@
     def put_v(b, o, blk):
         (vt_low, vt_high)[o][b] = blk.T
 
-    place(scal, (k0, k1, k2, k3), True, put_k)
-    place(scal, (v0, v1, v2, v3), False, put_v)
+    place(scal, (k0, k1, k2, k3), (v0, v1, v2, v3), put_k, put_v)
 
 
 def spread(row):
@@ -503,15 +507,17 @@
 
     mine = packed(o)
     other = swap(packed(1 - o), 2)
+    low, high = jnp.where(o == 0, mine, other), jnp.where(o == 0, other, mine)
+    main = jnp.concatenate([low[:BLK + PAD], high[:BLK + PAD], low[BLK + PAD:]], 0)
+    rest = high[BLK + PAD:]
+    main = jnp.stack([main] + [from_z(main, d) for d in (1, 2, 3)])
+    rest = jnp.stack([rest] + [from_y(rest, d) for d in (1, 2, 3)])
+    main, rest, queries = lax.optimization_barrier((main, rest, queries))
+    kp = [main] + [from_y(main, d) for d in (1, 2, 3)]
+    vp = [rest] + [from_z(rest, d) for d in (1, 2, 3)]
     qu = trade(jnp.concatenate([quarters(queries), quarters(upstream)], 1))
-    pair = jnp.stack([jnp.where(o == 0, mine, other), jnp.where(o == 0, other, mine)])
-    k_pair, v_pair = pair[:, :BLK + PAD], pair[:, BLK + PAD:]
-    k_line = jnp.stack([k_pair] + [from_z(k_pair, d) for d in (1, 2, 3)])
-    v_line = jnp.stack([v_pair] + [from_y(v_pair, d) for d in (1, 2, 3)])
-    k_line, v_line = lax.optimization_barrier((k_line, v_line))
-    kp = [k_line] + [from_y(k_line, d) for d in (1, 2, 3)]
-    vp = [v_line] + [from_z(v_line, d) for d in (1, 2, 3)]
-    starts = jnp.sum(total_of([k[:, :, BLK, :8] for k in kp]), (0, 1)).astype(jnp.int32)
+    counts = [k[:, r, :8] for k in kp for r in (BLK, 2 * BLK + PAD)]
+    starts = jnp.sum(total_of(counts), 0).astype(jnp.int32)
     bases = [BLK * (16 * (p >> 1) + 8 * (p & 1) + z % 2 * 4 + y) for p in range(4)]
     scal = jnp.concatenate([starts, jnp.stack(bases + [z, y, member, member]).astype(jnp.int32)])
     w = jnp.broadcast_to(

time: 233 us -> 247 us (1.060); the launches traced: 234 us -> 243 us
  Pallas kernels: 56.4 us -> 74.1 us
  waiting for transfers between devices: 67.5 us -> 56.3 us
  starting transfers between devices: 91.1 us -> 94.2 us
    pallas_call x4, Pallas kernels: 56.4 us -> 74.1 us  [call(): pl.pallas_call(kernel, grid=(4 if split else 1,), out_shape=tuple(shapes)...]
    ppermute x32, waiting for transfers between devices: 59.8 us -> 47.6 us  [send(): return lax.ppermute(x, CTX, pairs)]
  transfers between devices with their start and end apart: 34 -> 34, of which waited for: 15 -> 13; matrix products, arithmetic and copies ran while one was open for 4% -> 2% of each run, Pallas kernels for 10% -> 14%
where the time goes in v1:
time: 247 us; the launch traced here: 243 us
  starting transfers between devices  94.2 us (38%)
  Pallas kernels  74.1 us (30%)
  waiting for transfers between devices  56.3 us (23%)
  blocking collectives  5.95 us (2%)
  other arithmetic  5.8 us (2%)
  local copies, waits for them, and re-layouts  5.08 us (2%)
    ppermute x32, starting transfers between devices, send(): return lax.ppermute(x, CTX, pairs)  83.4 us
    pallas_call x4, Pallas kernels, call(): pl.pallas_call(kernel, grid=(4 if split else 1,), out_shape=tuple(shapes)...  74.1 us
    ppermute x32, waiting for transfers between devices, send(): return lax.ppermute(x, CTX, pairs)  47.6 us
    all_to_all x2, starting transfers between devices, trade(): return lax.all_to_all(x, GROUP, 0, 0, tiled=True)  10.8 us
    all_to_all x2, waiting for transfers between devices, trade(): return lax.all_to_all(x, GROUP, 0, 0, tiled=True)  8.68 us
    psum x1, blocking collectives, local(): lax.psum(critic[:, 0, :] - jnp.where(own, targets[None, :], 0.0), 'head')  5.95 us
  transfers between devices with their start and end apart: 34, of which 13 were waited for; matrix products, arithmetic and copies ran while one was open for 2% of the time, Pallas kernels for 14%

profile of v1, /device:TPU:0, one launch (start us, length us, event | category | flops | bytes accessed | tf_op | source)
XLA Modules:
  0.0 242.9 jit_solution(12075476689474096393)
XLA Ops:
  0.6 0.9 convert_reduce_fusion
  1.6 1.0 constant_dynamic-slice_fusion.3
  2.6 0.1 fusion.3
  2.7 3.2 %collective-permute-start = (bf16[528,128]{1,0:T(8,128)(2,1)S(1)}, bf16[528,128]{1,0:T(8,128)(2,1)S(1)}, u32[]{:S(2)}, u32[]{:S(2)}) collective-permute-start(bf16[528,128]{1,0:T(8,128)(2,1)S(1)} %fusion.3), channel_id=1, source_target_pairs={{0,16},{1,17},{2,18},{3,19},{4,20},{5,21},{6,22},{7,23},{8,24},{9,... | collective-permute-start | bytes 405512 | tf_op jit(solution)/shard_map/ppermute | solution.py:447
  5.9 3.6 %collective-permute-done = bf16[528,128]{1,0:T(8,128)(2,1)S(1)} collective-permute-done((bf16[528,128]{1,0:T(8,128)(2,1)S(1)}, bf16[528,128]{1,0:T(8,128)(2,1)S(1)}, u32[]{:S(2)}, u32[]{:S(2)}) %collective-permute-start) | collective-permute-done | bytes 135200 | tf_op jit(solution)/shard_map/ppermute | solution.py:447
  9.5 0.1 broadcast_select_fusion
  9.7 3.5 %collective-permute-start.5 = (bf16[256,128]{1,0:T(8,128)(2,1)S(1)}, bf16[256,128]{1,0:T(8,128)(2,1)S(1)}, u32[]{:S(2)}, u32[]{:S(2)}) collective-permute-start(bf16[256,128]{1,0:T(8,128)(2,1)S(1)} %get-tuple-element.157), channel_id=1, source_target_pairs={{0,2},{1,3},{2,0},{3,1},{4,6},{5,7},{6,4},{7,5},{8,10},{9,11},{10,... | collective-permute-start | bytes 196616 | tf_op jit(solution)/shard_map/ppermute | solution.py:447
  13.2 1.1 collective-permute-start.4
  14.3 1.0 collective-permute-start.6
  15.3 4.0 %collective-permute-start.2 = (bf16[800,128]{1,0:T(8,128)(2,1)S(1)}, bf16[800,128]{1,0:T(8,128)(2,1)S(1)}, u32[]{:S(2)}, u32[]{:S(2)}) collective-permute-start(bf16[800,128]{1,0:T(8,128)(2,1)S(1)} %get-tuple-element.155), channel_id=1, source_target_pairs={{0,8},{1,9},{2,10},{3,11},{4,12},{5,13},{6,14},{7,15},{8,0},{9,1},... | collective-permute-start | bytes 614408 | tf_op jit(solution)/shard_map/ppermute | solution.py:447
  19.2 0.7 collective-permute-start.1
  19.9 1.3 collective-permute-start.3
  21.4 3.8 %collective-permute-done.2 = bf16[800,128]{1,0:T(8,128)(2,1)S(1)} collective-permute-done((bf16[800,128]{1,0:T(8,128)(2,1)S(1)}, bf16[800,128]{1,0:T(8,128)(2,1)S(1)}, u32[]{:S(2)}, u32[]{:S(2)}) %collective-permute-start.2) | collective-permute-done | bytes 204832 | tf_op jit(solution)/shard_map/ppermute | solution.py:447
  25.2 2.5 %collective-permute-done.1 = bf16[800,128]{1,0:T(8,128)(2,1)S(1)} collective-permute-done((bf16[800,128]{1,0:T(8,128)(2,1)S(1)}, bf16[800,128]{1,0:T(8,128)(2,1)S(1)}, u32[]{:S(2)}, u32[]{:S(2)}) %collective-permute-start.1) | collective-permute-done | bytes 204832 | tf_op jit(solution)/shard_map/ppermute | solution.py:447
  28.0 1.5 maximum_maximum_fusion
  29.5 6.2 %all-to-all-start = ((bf16[4,512,512]{2,1,0:T(8,128)(2,1)}), bf16[4,512,512]{2,1,0:T(8,128)(2,1)}, u32[]{:S(2)}, u32[]{:S(2)}) async-start(bf16[4,512,512]{2,1,0:T(8,128)(2,1)} %maximum_maximum_fusion), calls=%async_computation | async-start | bytes 4194304 | tf_op jit(solution)/shard_map/all_to_all | solution.py:455
  35.7 0.7 collective-permute-start.9
  36.4 3.1 %collective-permute-start.8 = (bf16[4,800,128]{2,1,0:T(8,128)(2,1)S(1)}, bf16[4,800,128]{2,1,0:T(8,128)(2,1)}, u32[]{:S(2)}, u32[]{:S(2)}) collective-permute-start(bf16[4,800,128]{2,1,0:T(8,128)(2,1)S(1)} %pad_maximum_fusion.1.k0), channel_id=1, source_target_pairs={{0,2},{1,3},{2,0},{3,1},{4,6},{5,7},{6,4},{7,5},{8,10},{9,11},{10,... | collective-permute-start | bytes 2457608 | tf_op jit(solution)/shard_map/ppermute | solution.py:447
  39.4 1.0 collective-permute-start.12
  40.4 4.1 %collective-permute-start.11 = (bf16[4,256,128]{2,1,0:T(8,128)(2,1)S(1)}, bf16[4,256,128]{2,1,0:T(8,128)(2,1)S(1)}, u32[]{:S(2)}, u32[]{:S(2)}) collective-permute-start(bf16[4,256,128]{2,1,0:T(8,128)(2,1)S(1)} %pad_maximum_fusion.10.v0), channel_id=1, source_target_pairs={{0,8},{1,9},{2,10},{3,11},{4,12},{5,13},{6,14},{7,15},{8,0},{9,1},... | collective-permute-start | bytes 786440 | tf_op jit(solution)/shard_map/ppermute | solution.py:447
  44.6 13.0 %collective-permute-done.9.k3 = bf16[4,800,128]{2,1,0:T(8,128)(2,1)S(1)} collective-permute-done((bf16[4,800,128]{2,1,0:T(8,128)(2,1)S(1)}, bf16[4,800,128]{2,1,0:T(8,128)(2,1)S(1)}, u32[]{:S(2)}, u32[]{:S(2)}) %collective-permute-start.9) | collective-permute-done | bytes 819232 | tf_op jit(solution)/shard_map/ppermute | solution.py:447
  57.6 3.8 %collective-permute-start.10 = (bf16[4,256,128]{2,1,0:T(8,128)(2,1)S(1)}, bf16[4,256,128]{2,1,0:T(8,128)(2,1)S(1)}, u32[]{:S(2)}, u32[]{:S(2)}) collective-permute-start(bf16[4,256,128]{2,1,0:T(8,128)(2,1)S(1)} %pad_maximum_fusion.10.v0), channel_id=1, source_target_pairs={{0,12},{1,13},{2,14},{3,15},{4,0},{5,1},{6,2},{7,3},{8,4},{9,5},{1... | collective-permute-start | bytes 786440 | tf_op jit(solution)/shard_map/ppermute | solution.py:447
  61.4 0.8 dynamic_slice.23
  62.2 11.3 %collective-permute-done.8.k2 = bf16[4,800,128]{2,1,0:T(8,128)(2,1)} collective-permute-done((bf16[4,800,128]{2,1,0:T(8,128)(2,1)S(1)}, bf16[4,800,128]{2,1,0:T(8,128)(2,1)}, u32[]{:S(2)}, u32[]{:S(2)}) %collective-permute-start.8) | collective-permute-done | bytes 819232 | tf_op jit(solution)/shard_map/ppermute | solution.py:447
  73.6 0.8 fusion.14
  74.7 25.8 %attention_forward.1 = (bf16[4,4,128,256]{3,2,1,0:T(8,128)(2,1)}, f32[4,4,1,256]{3,2,1,0:T(1,128)S(1)}, f32[4,1,256]{2,1,0:T(1,128)S(1)}, bf16[4,4,128,256]{3,2,1,0:T(8,128)(2,1)}) custom-call(s32[16]{0:T(128)S(1)} %concatenate.58.scal, bf16[4,512,512]{2,1,0:T(8,128)(2,1)} %all-to-all-done.u_ref.q_ref, bf16[4,800,128]{2,1,0:T(8,128)(2,1)} %copy-done, ...), custom_call_target="tpu_custom_call" | custom-call | flops 8999999488 | bytes 8388608 | tf_op jit(solution)/shard_map/attention_forward/pallas_call | solution.py:376
  100.6 6.0 %psum.7 = f32[4,256]{1,0:T(4,128)S(1)} all-reduce(f32[4,256]{1,0:T(4,128)S(1)} %bitcast_subtract_fusion), channel_id=1, replica_groups=mesh['head'=4,'outer'=2,'zh'=2,'zl'=2,'y'=4] {'head'}, use_global_device_ids=true, to_apply=%region_2.3 | all-reduce | flops 1024 | bytes 8192 | tf_op jit(solution)/shard_map/psum | solution.py:532
  106.5 5.4 %collective-permute-start.15 = (f32[4,256]{1,0:T(4,128)S(1)}, f32[4,256]{1,0:T(4,128)S(1)}, u32[]{:S(2)}, u32[]{:S(2)}) collective-permute-start(f32[4,256]{1,0:T(4,128)S(1)} %psum.7), channel_id=1, source_target_pairs={{0,24},{1,25},{2,26},{3,27},{4,28},{5,29},{6,30},{7,31},{8,16},{9,... | collective-permute-start | bytes 12296 | tf_op jit(solution)/shard_map/ppermute | solution.py:447
  111.9 0.9 collective-permute-start.14
  112.8 0.5 collective-permute-start.13
  113.3 6.3 %prepare_backward.1 = (bf16[4,4,128,256]{3,2,1,0:T(8,128)(2,1)}, bf16[4096,128]{1,0:T(8,128)(2,1)}, bf16[4096,128]{1,0:T(8,128)(2,1)}, bf16[16,128,256]{2,1,0:T(...) custom-call(s32[16]{0:T(128)S(1)} %concatenate.58.scal, ...), custom_call_target="tpu_custom_call" | custom-call | flops 100000000 | bytes 8388608 | tf_op jit(solution)/shard_map/prepare_backward/pallas_call | solution.py:376
  119.7 14.2 %attention_upper.1 = (bf16[4,4,256,128]{3,2,1,0:T(8,128)(2,1)}, bf16[4,4,128,256]{3,2,1,0:T(8,128)(2,1)}, f32[4,4,1,256]{3,2,1,0:T(1,128)S(1)}, bf16[1040,256]{1...) custom-call(s32[16]{0:T(128)S(1)} %concatenate.58.scal, ...), custom_call_target="tpu_custom_call" | custom-call | flops 8000000000 | bytes 8388608 | tf_op jit(solution)/shard_map/attention_upper/pallas_call | solution.py:376
  133.9 5.2 %collective-permute-start.16 = (bf16[1040,256]{1,0:T(8,128)(2,1)S(1)}, bf16[1040,256]{1,0:T(8,128)(2,1)S(1)}, u32[]{:S(2)}, u32[]{:S(2)}) collective-permute-start(bf16[1040,256]{1,0:T(8,128)(2,1)S(1)} %get-tuple-element.69), channel_id=1, source_target_pairs={{0,1},{1,2},{2,3},{3,0},{4,5},{5,6},{6,7},{7,4},{8,9},{9,10},{10,1... | collective-permute-start | bytes 1597448 | tf_op jit(solution)/shard_map/ppermute | solution.py:447
  139.1 17.7 %collective-permute-start.17 = (bf16[1040,256]{1,0:T(8,128)(2,1)S(1)}, bf16[1040,256]{1,0:T(8,128)(2,1)S(1)}, u32[]{:S(2)}, u32[]{:S(2)}) collective-permute-start(bf16[1040,256]{1,0:T(8,128)(2,1)S(1)} %get-tuple-element.70), channel_id=1, source_target_pairs={{0,2},{1,3},{2,0},{3,1},{4,6},{5,7},{6,4},{7,5},{8,10},{9,11},{10,... | collective-permute-start | bytes 1597448 | tf_op jit(solution)/shard_map/ppermute | solution.py:447
  156.8 0.2 collective-permute-start.18
  157.0 27.8 %attention_lower.1 = (bf16[4,256,512]{2,1,0:T(8,128)(2,1)}, bf16[512,256]{1,0:T(8,128)(2,1)S(1)}, bf16[512,256]{1,0:T(8,128)(2,1)S(1)}, bf16[512,256]{1,0:T(8,12...) custom-call(s32[16]{0:T(128)S(1)} %concatenate.58.scal, ...), custom_call_target="tpu_custom_call" | custom-call | flops 16000000000 | bytes 8388608 | tf_op jit(solution)/shard_map/attention_lower/pallas_call | solution.py:376
  184.9 3.7 %collective-permute-start.19 = (bf16[512,256]{1,0:T(8,128)(2,1)S(1)}, bf16[512,256]{1,0:T(8,128)(2,1)S(1)}, u32[]{:S(2)}, u32[]{:S(2)}) collective-permute-start(bf16[512,256]{1,0:T(8,128)(2,1)S(1)} %get-tuple-element.86), channel_id=1, source_target_pairs={{0,1},{1,2},{2,3},{3,0},{4,5},{5,6},{6,7},{7,4},{8,9},{9,10},{10,1... | collective-permute-start | bytes 786440 | tf_op jit(solution)/shard_map/ppermute | solution.py:447
  188.6 5.7 %collective-permute-start.20 = (bf16[512,256]{1,0:T(8,128)(2,1)S(1)}, bf16[512,256]{1,0:T(8,128)(2,1)S(1)}, u32[]{:S(2)}, u32[]{:S(2)}) collective-permute-start(bf16[512,256]{1,0:T(8,128)(2,1)S(1)} %get-tuple-element.91), channel_id=1, source_target_pairs={{0,2},{1,3},{2,0},{3,1},{4,6},{5,7},{6,4},{7,5},{8,10},{9,11},{10,... | collective-permute-start | bytes 786440 | tf_op jit(solution)/shard_map/ppermute | solution.py:447
  194.3 2.9 %collective-permute-start.23 = (bf16[512,256]{1,0:T(8,128)(2,1)S(1)}, bf16[512,256]{1,0:T(8,128)(2,1)S(1)}, u32[]{:S(2)}, u32[]{:S(2)}) collective-permute-start(bf16[512,256]{1,0:T(8,128)(2,1)S(1)} %get-tuple-element.95), channel_id=1, source_target_pairs={{0,8},{1,9},{2,10},{3,11},{4,12},{5,13},{6,14},{7,15},{8,0},{9,1},... | collective-permute-start | bytes 786440 | tf_op jit(solution)/shard_map/ppermute | solution.py:447
  197.2 0.3 fusion.19
  197.5 1.8 collective-permute-done.19
  199.3 1.0 collective-permute-start.24
  200.3 3.7 %collective-permute-done.20 = bf16[512,256]{1,0:T(8,128)(2,1)S(1)} collective-permute-done((bf16[512,256]{1,0:T(8,128)(2,1)S(1)}, bf16[512,256]{1,0:T(8,128)(2,1)S(1)}, u32[]{:S(2)}, u32[]{:S(2)}) %collective-permute-start.20) | collective-permute-done | bytes 262176 | tf_op jit(solution)/shard_map/ppermute | solution.py:447
  203.9 3.0 %collective-permute-done.22 = bf16[512,256]{1,0:T(8,128)(2,1)S(1)} collective-permute-done((bf16[512,256]{1,0:T(8,128)(2,1)S(1)}, bf16[512,256]{1,0:T(8,128)(2,1)S(1)}, u32[]{:S(2)}, u32[]{:S(2)}) %collective-permute-start.22) | collective-permute-done | bytes 262176 | tf_op jit(solution)/shard_map/ppermute | solution.py:447
  207.0 0.3 collective-permute-done.24
  207.2 0.1 add_convert_fusion.1
  207.4 0.1 add_convert_fusion
  207.6 1.8 collective-permute-start.28
  209.4 1.5 collective-permute-start.30
  210.9 0.7 collective-permute-start.29
  211.6 2.2 collective-permute-start.25
  213.8 2.0 collective-permute-start.26
  215.8 1.7 collective-permute-start.27
  217.6 2.2 collective-permute-done.25
  219.8 2.2 collective-permute-done.26
  222.0 0.1 fusion.18
  222.2 2.9 %collective-permute-start.31 = (bf16[272,256]{1,0:T(8,128)(2,1)S(1)}, bf16[272,256]{1,0:T(8,128)(2,1)S(1)}, u32[]{:S(2)}, u32[]{:S(2)}) collective-permute-start(bf16[272,256]{1,0:T(8,128)(2,1)S(1)} %pad_maximum_fusion.14), channel_id=1, source_target_pairs={{0,16},{1,17},{2,18},{3,19},{4,20},{5,21},{6,22},{7,23},{8,24},{9,... | collective-permute-start | bytes 417800 | tf_op jit(solution)/shard_map/ppermute | solution.py:447
  225.2 0.6 constant_dynamic-slice_fusion
  225.7 4.6 %all-to-all-start.1 = ((bf16[4,256,512]{2,1,0:T(8,128)(2,1)}), bf16[4,256,512]{2,1,0:T(8,128)(2,1)S(1)}, u32[]{:S(2)}, u32[]{:S(2)}) async-start(bf16[4,256,512]{2,1,0:T(8,128)(2,1)} %get-tuple-element.88), calls=%async_computation.1 | async-start | bytes 2097152 | tf_op jit(solution)/shard_map/all_to_all | solution.py:455
  230.4 0.6 copy.17
  231.1 0.8 copy.15
  231.9 0.8 copy.14
  232.6 8.7 %all-to-all-done.1 = bf16[4,256,512]{2,1,0:T(8,128)(2,1)S(1)} async-done(((bf16[4,256,512]{2,1,0:T(8,128)(2,1)}), bf16[4,256,512]{2,1,0:T(8,128)(2,1)S(1)}, u32[]{:S(2)}, u32[]{:S(2)}) %all-to-all-start.1) | async-done | bytes 1048608 | tf_op jit(solution)/shard_map/all_to_all | solution.py:455
  241.4 1.1 pad_maximum_fusion
  (76 shorter events, 1.4 us)
Async XLA Ops:
  0.6 20.6 %copy-start.2 = (bf16[256,2048]{1,0:T(8,128)(2,1)S(1)}, bf16[256,2048]{1,0:T(8,128)(2,1)}, u32[]{:S(2)}) copy-start(bf16[256,2048]{1,0:T(8,128)(2,1)} %param.13) | copy-start | bytes 3145732
  2.7 6.8 %collective-permute-start = (bf16[528,128]{1,0:T(8,128)(2,1)S(1)}, bf16[528,128]{1,0:T(8,128)(2,1)S(1)}, u32[]{:S(2)}, u32[]{:S(2)}) collective-permute-start(bf16[528,128]{1,0:T(8,128)(2,1)S(1)} %fusion.3), channel_id=1, source_target_pairs={{0,16},{1,17},{2,18},{3,19},{4,20},{5,21},{6,22},{7,23},{8,24},{9,... | collective-permute-start | bytes 405512 | tf_op jit(solution)/shard_map/ppermute | solution.py:447
  9.7 10.2 %collective-permute-start.5 = (bf16[256,128]{1,0:T(8,128)(2,1)S(1)}, bf16[256,128]{1,0:T(8,128)(2,1)S(1)}, u32[]{:S(2)}, u32[]{:S(2)}) collective-permute-start(bf16[256,128]{1,0:T(8,128)(2,1)S(1)} %get-tuple-element.157), channel_id=1, source_target_pairs={{0,2},{1,3},{2,0},{3,1},{4,6},{5,7},{6,4},{7,5},{8,10},{9,11},{10,... | collective-permute-start | bytes 196616 | tf_op jit(solution)/shard_map/ppermute | solution.py:447
  13.2 8.1 %collective-permute-start.4 = (bf16[256,128]{1,0:T(8,128)(2,1)S(1)}, bf16[256,128]{1,0:T(8,128)(2,1)S(1)}, u32[]{:S(2)}, u32[]{:S(2)}) collective-permute-start(bf16[256,128]{1,0:T(8,128)(2,1)S(1)} %get-tuple-element.157), channel_id=1, source_target_pairs={{0,3},{1,0},{2,1},{3,2},{4,7},{5,4},{6,5},{7,6},{8,11},{9,8},{10,9... | collective-permute-start | bytes 196616 | tf_op jit(solution)/shard_map/ppermute | solution.py:447
  14.3 7.1 %collective-permute-start.6 = (bf16[256,128]{1,0:T(8,128)(2,1)S(1)}, bf16[256,128]{1,0:T(8,128)(2,1)S(1)}, u32[]{:S(2)}, u32[]{:S(2)}) collective-permute-start(bf16[256,128]{1,0:T(8,128)(2,1)S(1)} %get-tuple-element.157), channel_id=1, source_target_pairs={{0,1},{1,2},{2,3},{3,0},{4,5},{5,6},{6,7},{7,4},{8,9},{9,10},{10,1... | collective-permute-start | bytes 196616 | tf_op jit(solution)/shard_map/ppermute | solution.py:447
  15.3 12.6 %copy-start.3 = (bf16[256,2048]{1,0:T(8,128)(2,1)S(1)}, bf16[256,2048]{1,0:T(8,128)(2,1)}, u32[]{:S(2)}) copy-start(bf16[256,2048]{1,0:T(8,128)(2,1)} %param.7) | copy-start | bytes 3145732
  15.3 10.0 %collective-permute-start.2 = (bf16[800,128]{1,0:T(8,128)(2,1)S(1)}, bf16[800,128]{1,0:T(8,128)(2,1)S(1)}, u32[]{:S(2)}, u32[]{:S(2)}) collective-permute-start(bf16[800,128]{1,0:T(8,128)(2,1)S(1)} %get-tuple-element.155), channel_id=1, source_target_pairs={{0,8},{1,9},{2,10},{3,11},{4,12},{5,13},{6,14},{7,15},{8,0},{9,1},... | collective-permute-start | bytes 614408 | tf_op jit(solution)/shard_map/ppermute | solution.py:447
  19.2 8.5 %collective-permute-start.1 = (bf16[800,128]{1,0:T(8,128)(2,1)S(1)}, bf16[800,128]{1,0:T(8,128)(2,1)S(1)}, u32[]{:S(2)}, u32[]{:S(2)}) collective-permute-start(bf16[800,128]{1,0:T(8,128)(2,1)S(1)} %get-tuple-element.155), channel_id=1, source_target_pairs={{0,12},{1,13},{2,14},{3,15},{4,0},{5,1},{6,2},{7,3},{8,4},{9,5},{1... | collective-permute-start | bytes 614408 | tf_op jit(solution)/shard_map/ppermute | solution.py:447
  19.9 7.8 %collective-permute-start.3 = (bf16[800,128]{1,0:T(8,128)(2,1)S(1)}, bf16[800,128]{1,0:T(8,128)(2,1)S(1)}, u32[]{:S(2)}, u32[]{:S(2)}) collective-permute-start(bf16[800,128]{1,0:T(8,128)(2,1)S(1)} %get-tuple-element.155), channel_id=1, source_target_pairs={{0,4},{1,5},{2,6},{3,7},{4,8},{5,9},{6,10},{7,11},{8,12},{9,13},{1... | collective-permute-start | bytes 614408 | tf_op jit(solution)/shard_map/ppermute | solution.py:447
  27.9 45.8 %copy-start = (bf16[4,800,128]{2,1,0:T(8,128)(2,1)}, bf16[4,800,128]{2,1,0:T(8,128)(2,1)S(1)}, u32[]{:S(2)}) copy-start(bf16[4,800,128]{2,1,0:T(8,128)(2,1)S(1)} %pad_maximum_fusion.1.k0) | copy-start | bytes 2457604
  29.5 45.0 %all-to-all-start = ((bf16[4,512,512]{2,1,0:T(8,128)(2,1)}), bf16[4,512,512]{2,1,0:T(8,128)(2,1)}, u32[]{:S(2)}, u32[]{:S(2)}) async-start(bf16[4,512,512]{2,1,0:T(8,128)(2,1)} %maximum_maximum_fusion), calls=%async_computation | async-start | bytes 4194304 | tf_op jit(solution)/shard_map/all_to_all | solution.py:455
  35.7 21.9 %collective-permute-start.9 = (bf16[4,800,128]{2,1,0:T(8,128)(2,1)S(1)}, bf16[4,800,128]{2,1,0:T(8,128)(2,1)S(1)}, u32[]{:S(2)}, u32[]{:S(2)}) collective-permute-start(bf16[4,800,128]{2,1,0:T(8,128)(2,1)S(1)} %pad_maximum_fusion.1.k0), channel_id=1, source_target_pairs={{0,1},{1,2},{2,3},{3,0},{4,5},{5,6},{6,7},{7,4},{8,9},{9,10},{10,1... | collective-permute-start | bytes 2457608 | tf_op jit(solution)/shard_map/ppermute | solution.py:447
  36.4 37.1 %collective-permute-start.8 = (bf16[4,800,128]{2,1,0:T(8,128)(2,1)S(1)}, bf16[4,800,128]{2,1,0:T(8,128)(2,1)}, u32[]{:S(2)}, u32[]{:S(2)}) collective-permute-start(bf16[4,800,128]{2,1,0:T(8,128)(2,1)S(1)} %pad_maximum_fusion.1.k0), channel_id=1, source_target_pairs={{0,2},{1,3},{2,0},{3,1},{4,6},{5,7},{6,4},{7,5},{8,10},{9,11},{10,... | collective-permute-start | bytes 2457608 | tf_op jit(solution)/shard_map/ppermute | solution.py:447
  39.4 34.2 %collective-permute-start.7 = (bf16[4,800,128]{2,1,0:T(8,128)(2,1)S(1)}, bf16[4,800,128]{2,1,0:T(8,128)(2,1)}, u32[]{:S(2)}, u32[]{:S(2)}) collective-permute-start(bf16[4,800,128]{2,1,0:T(8,128)(2,1)S(1)} %pad_maximum_fusion.1.k0), channel_id=1, source_target_pairs={{0,3},{1,0},{2,1},{3,2},{4,7},{5,4},{6,5},{7,6},{8,11},{9,8},{10,9... | collective-permute-start | bytes 2457608 | tf_op jit(solution)/shard_map/ppermute | solution.py:447
  39.4 35.1 %collective-permute-start.12 = (bf16[4,256,128]{2,1,0:T(8,128)(2,1)S(1)}, bf16[4,256,128]{2,1,0:T(8,128)(2,1)S(1)}, u32[]{:S(2)}, u32[]{:S(2)}) collective-permute-start(bf16[4,256,128]{2,1,0:T(8,128)(2,1)S(1)} %pad_maximum_fusion.10.v0), channel_id=1, source_target_pairs={{0,4},{1,5},{2,6},{3,7},{4,8},{5,9},{6,10},{7,11},{8,12},{9,13},{1... | collective-permute-start | bytes 786440 | tf_op jit(solution)/shard_map/ppermute | solution.py:447
  40.4 34.1 %collective-permute-start.11 = (bf16[4,256,128]{2,1,0:T(8,128)(2,1)S(1)}, bf16[4,256,128]{2,1,0:T(8,128)(2,1)S(1)}, u32[]{:S(2)}, u32[]{:S(2)}) collective-permute-start(bf16[4,256,128]{2,1,0:T(8,128)(2,1)S(1)} %pad_maximum_fusion.10.v0), channel_id=1, source_target_pairs={{0,8},{1,9},{2,10},{3,11},{4,12},{5,13},{6,14},{7,15},{8,0},{9,1},... | collective-permute-start | bytes 786440 | tf_op jit(solution)/shard_map/ppermute | solution.py:447
  57.6 17.1 %copy-start.4 = (bf16[4,800,128]{2,1,0:T(8,128)(2,1)}, bf16[4,800,128]{2,1,0:T(8,128)(2,1)S(1)}, u32[]{:S(2)}) copy-start(bf16[4,800,128]{2,1,0:T(8,128)(2,1)S(1)} %collective-permute-done.9.k3) | copy-start | bytes 2457604
  57.6 16.9 %collective-permute-start.10 = (bf16[4,256,128]{2,1,0:T(8,128)(2,1)S(1)}, bf16[4,256,128]{2,1,0:T(8,128)(2,1)S(1)}, u32[]{:S(2)}, u32[]{:S(2)}) collective-permute-start(bf16[4,256,128]{2,1,0:T(8,128)(2,1)S(1)} %pad_maximum_fusion.10.v0), channel_id=1, source_target_pairs={{0,12},{1,13},{2,14},{3,15},{4,0},{5,1},{6,2},{7,3},{8,4},{9,5},{1... | collective-permute-start | bytes 786440 | tf_op jit(solution)/shard_map/ppermute | solution.py:447
  74.7 25.8 %copy-start.5 = (f32[256]{0:T(256)S(1)}, f32[256]{0:T(256)}, u32[]{:S(2)}) copy-start(f32[256]{0:T(256)} %param.12) | copy-start | bytes 3076
  74.7 38.6 %copy-start.1 = (bf16[4,800,128]{2,1,0:T(8,128)(2,1)S(1)}, bf16[4,800,128]{2,1,0:T(8,128)(2,1)}, u32[]{:S(2)}) copy-start(bf16[4,800,128]{2,1,0:T(8,128)(2,1)} %copy-done) | copy-start | bytes 2457604
  106.5 13.1 %collective-permute-start.15 = (f32[4,256]{1,0:T(4,128)S(1)}, f32[4,256]{1,0:T(4,128)S(1)}, u32[]{:S(2)}, u32[]{:S(2)}) collective-permute-start(f32[4,256]{1,0:T(4,128)S(1)} %psum.7), channel_id=1, source_target_pairs={{0,24},{1,25},{2,26},{3,27},{4,28},{5,29},{6,30},{7,31},{8,16},{9,... | collective-permute-start | bytes 12296 | tf_op jit(solution)/shard_map/ppermute | solution.py:447
  111.9 7.7 %collective-permute-start.14 = (f32[4,256]{1,0:T(4,128)S(1)}, f32[4,256]{1,0:T(4,128)S(1)}, u32[]{:S(2)}, u32[]{:S(2)}) collective-permute-start(f32[4,256]{1,0:T(4,128)S(1)} %psum.7), channel_id=1, source_target_pairs={{0,16},{1,17},{2,18},{3,19},{4,20},{5,21},{6,22},{7,23},{8,24},{9,... | collective-permute-start | bytes 12296 | tf_op jit(solution)/shard_map/ppermute | solution.py:447
  112.8 6.8 %collective-permute-start.13 = (f32[4,256]{1,0:T(4,128)S(1)}, f32[4,256]{1,0:T(4,128)S(1)}, u32[]{:S(2)}, u32[]{:S(2)}) collective-permute-start(f32[4,256]{1,0:T(4,128)S(1)} %psum.7), channel_id=1, source_target_pairs={{0,8},{1,9},{2,10},{3,11},{4,12},{5,13},{6,14},{7,15},{8,0},{9,1},... | collective-permute-start | bytes 12296 | tf_op jit(solution)/shard_map/ppermute | solution.py:447
  133.9 50.9 %collective-permute-start.16 = (bf16[1040,256]{1,0:T(8,128)(2,1)S(1)}, bf16[1040,256]{1,0:T(8,128)(2,1)S(1)}, u32[]{:S(2)}, u32[]{:S(2)}) collective-permute-start(bf16[1040,256]{1,0:T(8,128)(2,1)S(1)} %get-tuple-element.69), channel_id=1, source_target_pairs={{0,1},{1,2},{2,3},{3,0},{4,5},{5,6},{6,7},{7,4},{8,9},{9,10},{10,1... | collective-permute-start | bytes 1597448 | tf_op jit(solution)/shard_map/ppermute | solution.py:447
  139.1 45.7 %collective-permute-start.17 = (bf16[1040,256]{1,0:T(8,128)(2,1)S(1)}, bf16[1040,256]{1,0:T(8,128)(2,1)S(1)}, u32[]{:S(2)}, u32[]{:S(2)}) collective-permute-start(bf16[1040,256]{1,0:T(8,128)(2,1)S(1)} %get-tuple-element.70), channel_id=1, source_target_pairs={{0,2},{1,3},{2,0},{3,1},{4,6},{5,7},{6,4},{7,5},{8,10},{9,11},{10,... | collective-permute-start | bytes 1597448 | tf_op jit(solution)/shard_map/ppermute | solution.py:447
  156.8 28.1 %collective-permute-start.18 = (bf16[1040,256]{1,0:T(8,128)(2,1)}, bf16[1040,256]{1,0:T(8,128)(2,1)S(1)}, u32[]{:S(2)}, u32[]{:S(2)}) collective-permute-start(bf16[1040,256]{1,0:T(8,128)(2,1)} %get-tuple-element.71), channel_id=1, source_target_pairs={{0,3},{1,0},{2,1},{3,2},{4,7},{5,4},{6,5},{7,6},{8,11},{9,8},{10,9... | collective-permute-start | bytes 1597448 | tf_op jit(solution)/shard_map/ppermute | solution.py:447
  184.8 14.4 %copy-start.6 = (bf16[512,256]{1,0:T(8,128)(2,1)S(1)}, bf16[512,256]{1,0:T(8,128)(2,1)}, u32[]{:S(2)}) copy-start(bf16[512,256]{1,0:T(8,128)(2,1)} %get-tuple-element.96) | copy-start | bytes 786436
  184.9 14.4 %collective-permute-start.19 = (bf16[512,256]{1,0:T(8,128)(2,1)S(1)}, bf16[512,256]{1,0:T(8,128)(2,1)S(1)}, u32[]{:S(2)}, u32[]{:S(2)}) collective-permute-start(bf16[512,256]{1,0:T(8,128)(2,1)S(1)} %get-tuple-element.86), channel_id=1, source_target_pairs={{0,1},{1,2},{2,3},{3,0},{4,5},{5,6},{6,7},{7,4},{8,9},{9,10},{10,1... | collective-permute-start | bytes 786440 | tf_op jit(solution)/shard_map/ppermute | solution.py:447
  188.6 15.4 %collective-permute-start.20 = (bf16[512,256]{1,0:T(8,128)(2,1)S(1)}, bf16[512,256]{1,0:T(8,128)(2,1)S(1)}, u32[]{:S(2)}, u32[]{:S(2)}) collective-permute-start(bf16[512,256]{1,0:T(8,128)(2,1)S(1)} %get-tuple-element.91), channel_id=1, source_target_pairs={{0,2},{1,3},{2,0},{3,1},{4,6},{5,7},{6,4},{7,5},{8,10},{9,11},{10,... | collective-permute-start | bytes 786440 | tf_op jit(solution)/shard_map/ppermute | solution.py:447
  194.3 9.6 %collective-permute-start.21 = (bf16[512,256]{1,0:T(8,128)(2,1)S(1)}, bf16[512,256]{1,0:T(8,128)(2,1)S(1)}, u32[]{:S(2)}, u32[]{:S(2)}) collective-permute-start(bf16[512,256]{1,0:T(8,128)(2,1)S(1)} %get-tuple-element.92), channel_id=1, source_target_pairs={{0,3},{1,0},{2,1},{3,2},{4,7},{5,4},{6,5},{7,6},{8,11},{9,8},{10,9... | collective-permute-start | bytes 786440 | tf_op jit(solution)/shard_map/ppermute | solution.py:447
  194.3 12.7 %collective-permute-start.22 = (bf16[512,256]{1,0:T(8,128)(2,1)S(1)}, bf16[512,256]{1,0:T(8,128)(2,1)S(1)}, u32[]{:S(2)}, u32[]{:S(2)}) collective-permute-start(bf16[512,256]{1,0:T(8,128)(2,1)S(1)} %get-tuple-element.94), channel_id=1, source_target_pairs={{0,4},{1,5},{2,6},{3,7},{4,8},{5,9},{6,10},{7,11},{8,12},{9,13},{1... | collective-permute-start | bytes 786440 | tf_op jit(solution)/shard_map/ppermute | solution.py:447
  194.3 12.7 %collective-permute-start.23 = (bf16[512,256]{1,0:T(8,128)(2,1)S(1)}, bf16[512,256]{1,0:T(8,128)(2,1)S(1)}, u32[]{:S(2)}, u32[]{:S(2)}) collective-permute-start(bf16[512,256]{1,0:T(8,128)(2,1)S(1)} %get-tuple-element.95), channel_id=1, source_target_pairs={{0,8},{1,9},{2,10},{3,11},{4,12},{5,13},{6,14},{7,15},{8,0},{9,1},... | collective-permute-start | bytes 786440 | tf_op jit(solution)/shard_map/ppermute | solution.py:447
  199.3 8.0 %collective-permute-start.24 = (bf16[512,256]{1,0:T(8,128)(2,1)S(1)}, bf16[512,256]{1,0:T(8,128)(2,1)S(1)}, u32[]{:S(2)}, u32[]{:S(2)}) collective-permute-start(bf16[512,256]{1,0:T(8,128)(2,1)S(1)} %copy-done.6), channel_id=1, source_target_pairs={{0,12},{1,13},{2,14},{3,15},{4,0},{5,1},{6,2},{7,3},{8,4},{9,5},{1... | collective-permute-start | bytes 786440 | tf_op jit(solution)/shard_map/ppermute | solution.py:447
  207.6 8.2 %collective-permute-start.28 = (bf16[128,256]{1,0:T(8,128)(2,1)S(1)}, bf16[128,256]{1,0:T(8,128)(2,1)S(1)}, u32[]{:S(2)}, u32[]{:S(2)}) collective-permute-start(bf16[128,256]{1,0:T(8,128)(2,1)S(1)} %get-tuple-element.147), channel_id=1, source_target_pairs={{0,1},{1,2},{2,3},{3,0},{4,5},{5,6},{6,7},{7,4},{8,9},{9,10},{10,1... | collective-permute-start | bytes 196616 | tf_op jit(solution)/shard_map/ppermute | solution.py:447
  209.4 8.1 %collective-permute-start.30 = (bf16[128,256]{1,0:T(8,128)(2,1)S(1)}, bf16[128,256]{1,0:T(8,128)(2,1)S(1)}, u32[]{:S(2)}, u32[]{:S(2)}) collective-permute-start(bf16[128,256]{1,0:T(8,128)(2,1)S(1)} %get-tuple-element.148), channel_id=1, source_target_pairs={{0,3},{1,0},{2,1},{3,2},{4,7},{5,4},{6,5},{7,6},{8,11},{9,8},{10,9... | collective-permute-start | bytes 196616 | tf_op jit(solution)/shard_map/ppermute | solution.py:447
  210.9 6.6 %collective-permute-start.29 = (bf16[128,256]{1,0:T(8,128)(2,1)S(1)}, bf16[128,256]{1,0:T(8,128)(2,1)S(1)}, u32[]{:S(2)}, u32[]{:S(2)}) collective-permute-start(bf16[128,256]{1,0:T(8,128)(2,1)S(1)} %get-tuple-element.149), channel_id=1, source_target_pairs={{0,2},{1,3},{2,0},{3,1},{4,6},{5,7},{6,4},{7,5},{8,10},{9,11},{10,... | collective-permute-start | bytes 196616 | tf_op jit(solution)/shard_map/ppermute | solution.py:447
  211.6 8.2 %collective-permute-start.25 = (bf16[400,256]{1,0:T(8,128)(2,1)S(1)}, bf16[400,256]{1,0:T(8,128)(2,1)S(1)}, u32[]{:S(2)}, u32[]{:S(2)}) collective-permute-start(bf16[400,256]{1,0:T(8,128)(2,1)S(1)} %get-tuple-element.166), channel_id=1, source_target_pairs={{0,4},{1,5},{2,6},{3,7},{4,8},{5,9},{6,10},{7,11},{8,12},{9,13},{1... | collective-permute-start | bytes 614408 | tf_op jit(solution)/shard_map/ppermute | solution.py:447
  213.8 8.2 %collective-permute-start.26 = (bf16[400,256]{1,0:T(8,128)(2,1)S(1)}, bf16[400,256]{1,0:T(8,128)(2,1)S(1)}, u32[]{:S(2)}, u32[]{:S(2)}) collective-permute-start(bf16[400,256]{1,0:T(8,128)(2,1)S(1)} %get-tuple-element.167), channel_id=1, source_target_pairs={{0,8},{1,9},{2,10},{3,11},{4,12},{5,13},{6,14},{7,15},{8,0},{9,1},... | collective-permute-start | bytes 614408 | tf_op jit(solution)/shard_map/ppermute | solution.py:447
  215.8 6.2 %collective-permute-start.27 = (bf16[400,256]{1,0:T(8,128)(2,1)S(1)}, bf16[400,256]{1,0:T(8,128)(2,1)S(1)}, u32[]{:S(2)}, u32[]{:S(2)}) collective-permute-start(bf16[400,256]{1,0:T(8,128)(2,1)S(1)} %get-tuple-element.168), channel_id=1, source_target_pairs={{0,12},{1,13},{2,14},{3,15},{4,0},{5,1},{6,2},{7,3},{8,4},{9,5},{1... | collective-permute-start | bytes 614408 | tf_op jit(solution)/shard_map/ppermute | solution.py:447
  222.2 8.1 %collective-permute-start.31 = (bf16[272,256]{1,0:T(8,128)(2,1)S(1)}, bf16[272,256]{1,0:T(8,128)(2,1)S(1)}, u32[]{:S(2)}, u32[]{:S(2)}) collective-permute-start(bf16[272,256]{1,0:T(8,128)(2,1)S(1)} %pad_maximum_fusion.14), channel_id=1, source_target_pairs={{0,16},{1,17},{2,18},{3,19},{4,20},{5,21},{6,22},{7,23},{8,24},{9,... | collective-permute-start | bytes 417800 | tf_op jit(solution)/shard_map/ppermute | solution.py:447
  225.7 15.6 %all-to-all-start.1 = ((bf16[4,256,512]{2,1,0:T(8,128)(2,1)}), bf16[4,256,512]{2,1,0:T(8,128)(2,1)S(1)}, u32[]{:S(2)}, u32[]{:S(2)}) async-start(bf16[4,256,512]{2,1,0:T(8,128)(2,1)} %get-tuple-element.88), calls=%async_computation.1 | async-start | bytes 2097152 | tf_op jit(solution)/shard_map/all_to_all | solution.py:455
